TPU v7x, 128 devices: a whole 4x4x4 slice. The times are simulated.
128 devices in a mesh: grp: 16 (over y_hi, z, core), tp: 8 (over y_lo, x).
Axes of the slice: x: 4, y: 4 (y_hi: 2, y_lo: 2; y = y_hi * 2 + y_lo), z: 4, core: 2. Of those that a mesh axis runs over, the one named last changes fastest.
Arguments:
- hidden: bfloat16 [1024, 5120], P('grp', 'tp'), may hold values from -8 to 8
- query_key_value_weight: bfloat16 [5120, 10240], P(('grp', 'tp')), as said below
- w_out: bfloat16 [8192, 5120], P(None, ('grp', 'tp')), may hold values from -0.0625 to 0.0625
- k_cache: bfloat16 [128, 4096, 8, 128], P('grp', None, 'tp'), may hold values from -256 to 256
- value_cache: bfloat16 [128, 4096, 8, 128], P('grp', None, 'tp'), may hold values from -6 to 6
- lengths: int32 [1024], P('grp'), may hold values from 1 to 4096, as said below
- assign: int32 [1024], P('grp'), may hold values from 0 to 7, as said below
Outputs:
- attended: bfloat16 [1024, 5120], P('grp', 'tp')
Inputs may be any that keep to these rules, and one draw needn't show every extreme that they name: `lengths`: some row has length 4096. `assign`: within each rollout group's 64 rows every prompt is named by exactly 8 rows. `query_key_value_weight`: entries lie within 6 / sqrt(5120) of zero.
All inputs are finite; a program needn't handle non-finite values.
Results may differ from a plain program's by a relative error of at most 0.007.
Values may be sent and summed in bfloat16 or wider, within the bound.
A program may use at most 192 MiB of HBM per device.

v0:
```python
import jax
import jax.numpy as jnp
from jax import lax
from jax.sharding import PartitionSpec as P

QUERY_HEADS = 64
KEY_VALUE_HEADS = 8
HEAD_SIZE = 128


EPS = 1e-06
ROPE_BASE = 1000000.0


def head_norm(vec):
    return vec * lax.rsqrt(jnp.mean(vec * vec, axis=-1, keepdims=True) + EPS)


def rotate(vec, positions):
    half = vec.shape[-1] // 2
    freq = ROPE_BASE ** (-jnp.arange(half, dtype=jnp.float32) * 2.0 / vec.shape[-1])
    angle = positions.astype(jnp.float32)[:, None] * freq[None, :]
    angle = angle.reshape((angle.shape[0],) + (1,) * (vec.ndim - 2) + (half,))
    cosine, sine = (jnp.cos(angle), jnp.sin(angle))
    first, second = (vec[..., :half], vec[..., half:])
    return jnp.concatenate(
        [first * cosine - second * sine, second * cosine + first * sine], axis=-1
    )


def local(hidden, query_key_value_weight, w_out, k_cache, value_cache, lengths, assign):
    tp_count = lax.axis_size("tp")
    grp_count = lax.axis_size("grp")
    full = lax.all_gather(hidden, "tp", axis=1, tiled=True)
    values32 = full.astype(jnp.float32)
    normed_rows = (
        values32 * lax.rsqrt(jnp.mean(values32 * values32, axis=-1, keepdims=True) + EPS)
    ).astype(jnp.bfloat16)
    row_count, width = normed_rows.shape
    piece_rows = query_key_value_weight.shape[0]
    grown = lax.all_gather(query_key_value_weight, "grp", axis=0, tiled=True)
    columns = lax.all_to_all(grown, "tp", split_axis=1, concat_axis=0, tiled=True)
    permuted = (
        normed_rows.reshape(row_count, grp_count, tp_count, piece_rows)
        .transpose(0, 2, 1, 3)
        .reshape(row_count, width)
    )
    projected_rows = jnp.dot(permuted, columns, preferred_element_type=jnp.float32)
    head_group = QUERY_HEADS // KEY_VALUE_HEADS
    kv_local = projected_rows.shape[1] // ((head_group + 2) * HEAD_SIZE)
    blocks = projected_rows.reshape(row_count, kv_local, head_group + 2, HEAD_SIZE)
    query_rows = rotate(head_norm(blocks[:, :, :head_group]), lengths).astype(jnp.bfloat16)
    fresh_key_rows = rotate(head_norm(blocks[:, :, head_group]), lengths).astype(jnp.bfloat16)
    fresh_value_rows = blocks[:, :, head_group + 1].astype(jnp.bfloat16)
    sort_order = jnp.argsort(assign, stable=True)
    back = jnp.argsort(sort_order, stable=True)
    prompts = k_cache.shape[0]
    samples = row_count // prompts
    context = k_cache.shape[1]
    ordered_query_rows = query_rows[sort_order].reshape(
        prompts, samples, kv_local, head_group, HEAD_SIZE
    )
    ordered_key_rows = fresh_key_rows[sort_order].reshape(prompts, samples, kv_local, HEAD_SIZE)
    ordered_value_rows = fresh_value_rows[sort_order].reshape(prompts, samples, kv_local, HEAD_SIZE)
    sorted_lens = lengths[sort_order].reshape(prompts, samples)
    scale = HEAD_SIZE ** (-0.5)
    scores = (
        jnp.einsum(
            "pskjd,pckd->pskjc", ordered_query_rows, k_cache, preferred_element_type=jnp.float32
        )
        * scale
    )
    own = (
        jnp.einsum(
            "pskjd,pskd->pskj",
            ordered_query_rows,
            ordered_key_rows,
            preferred_element_type=jnp.float32,
        )
        * scale
    )
    mask = (jnp.arange(context, dtype=jnp.int32)[None, None, :] < sorted_lens[:, :, None])[
        :, :, None, None, :
    ]
    scores = jnp.where(mask, scores, -jnp.inf)
    top = jnp.maximum(jnp.max(scores, axis=-1), own)
    expo = jnp.where(mask, jnp.exp(scores - top[..., None]), 0.0)
    own_expo = jnp.exp(own - top)
    total = jnp.sum(expo, axis=-1) + own_expo
    weights = (expo / total[..., None]).astype(jnp.bfloat16)
    own_weight = (own_expo / total).astype(jnp.bfloat16)
    mixed = jnp.einsum(
        "pskjc,pckd->pskjd", weights, value_cache, preferred_element_type=jnp.float32
    )
    mixed = (
        mixed
        + own_weight.astype(jnp.float32)[..., None]
        * ordered_value_rows.astype(jnp.float32)[:, :, :, None, :]
    )
    attn = mixed.astype(jnp.bfloat16).reshape(row_count, kv_local * head_group * HEAD_SIZE)[back]
    piece_cols = w_out.shape[1]
    grown_out = lax.all_gather(w_out, "grp", axis=1, tiled=True)
    out_rows = lax.all_to_all(grown_out, "tp", split_axis=0, concat_axis=1, tiled=True)
    shuffled = jnp.dot(attn, out_rows, preferred_element_type=jnp.float32)
    partial_value = (
        shuffled.reshape(row_count, tp_count, grp_count, piece_cols)
        .transpose(0, 2, 1, 3)
        .reshape(row_count, width)
    )
    return lax.psum_scatter(partial_value, "tp", scatter_dimension=1, tiled=True).astype(
        jnp.bfloat16
    )


def solution(mesh):
    return jax.shard_map(
        local,
        mesh=mesh,
        in_specs=(
            P("grp", "tp"),
            P(("grp", "tp"), None),
            P(None, ("grp", "tp")),
            P("grp", None, "tp", None),
            P("grp", None, "tp", None),
            P("grp"),
            P("grp"),
        ),
        out_specs=P("grp", "tp"),
        check_vma=False,
    )
```

profile of v0, /device:TPU:20, one launch (start us, length us, event | category | flops | bytes accessed | tf_op | source)
XLA Modules:
  0.0 592.4 jit_solution(4635569396757251562)
XLA Ops:
  6.5 0.7 all-gather.3.cloned.1.call-update
  7.3 0.7 all-gather.5.cloned.1.call-update
  8.0 94.7 %all-gather.3.cloned.1.call-done = bf16[640,10240]{1,0:T(8,128)(2,1)} async-done(((bf16[40,10240]{1,0:T(8,128)(2,1)}), bf16[640,10240]{1,0:T(8,128)(2,1)}) %all-gather.3.cloned.1.call-update) | async-done | bytes 13107216 | tf_op jit(solution)/shard_map/all_gather | solution.py:41
  102.7 17.8 %copy.51 = bf16[640,10240]{0,1:T(8,128)(2,1)} copy(bf16[640,10240]{1,0:T(8,128)(2,1)} %all-gather.3.cloned.1.call-done) | data formatting | bytes 26214400 | tf_op jit(solution)/shard_map/all_gather | solution.py:41
  120.5 17.6 %copy.52 = bf16[640,8,1280]{2,0,1:T(8,128)(2,1)} copy(bf16[640,8,1280]{0,2,1:T(8,128)(2,1)} %bitcast.135) | data formatting | bytes 26214400 | tf_op jit(solution)/shard_map/all_to_all | solution.py:42
  138.1 6.4 %all-to-all-start = ((bf16[640,8,1280]{2,0,1:T(8,128)(2,1)}), bf16[640,8,1280]{2,0,1:T(8,128)(2,1)}, u32[]{:S(2)}, u32[]{:S(2)}) async-start(bf16[640,8,1280]{2,0,1:T(8,128)(2,1)} %copy.52), calls=%async_computation | async-start | bytes 26214400 | tf_op jit(solution)/shard_map/all_to_all | solution.py:42
  144.7 219.8 %all_gather.9 = bf16[64,5120]{0,1:T(8,128)(2,1)S(1)} all-gather(bf16[64,640]{0,1:T(8,128)(2,1)S(1)} %copy.49), channel_id=1, replica_groups=mesh['grp'=16,'tp'=8] {'tp'}, dimensions={1}, use_global_device_ids=true | all-gather | bytes 737280 | tf_op jit(solution)/shard_map/all_gather | solution.py:34
  365.2 14.4 %copy.56 = bf16[8192,640]{1,0:T(8,128)(2,1)} copy(bf16[8192,640]{0,1:T(8,128)(2,1)} %all-gather.5.cloned.1.call-done) | data formatting | bytes 20971520 | tf_op jit(solution)/shard_map/all_gather | solution.py:102
  379.5 15.1 %copy.57 = bf16[8,1024,640]{1,2,0:T(8,128)(2,1)} copy(bf16[8,1024,640]{2,1,0:T(8,128)(2,1)} %bitcast.136) | data formatting | bytes 20971520 | tf_op jit(solution)/shard_map/all_to_all | solution.py:103
  394.7 7.0 %all-to-all-start.1 = ((bf16[8,1024,640]{1,2,0:T(8,128)(2,1)}), bf16[8,1024,640]{1,2,0:T(8,128)(2,1)}, u32[]{:S(2)}, u32[]{:S(2)}) async-start(bf16[8,1024,640]{1,2,0:T(8,128)(2,1)} %copy.57), calls=%async_computation.1 | async-start | bytes 20971520 | tf_op jit(solution)/shard_map/all_to_all | solution.py:103
  402.1 2.0 sort.31
  404.2 0.8 gather_fusion
  405.1 2.0 sort.32
  407.5 17.7 %copy.53 = bf16[5120,1280]{0,1:T(8,128)(2,1)} copy(bf16[5120,1280]{1,0:T(8,128)(2,1)} %bitcast.6) | data formatting | bytes 26214400 | tf_op jit(solution)/shard_map/all_to_all | solution.py:42
  425.2 7.3 %convolution_bitcast_fusion.1 = f32[64,1,10,128]{3,0,2,1:T(8,128)S(1)} fusion(bf16[64,5120,1]{0,1,2:T(8,128)(2,1)S(1)} %bitcast.139, bf16[10,128,5120]{2,1,0:T(8,128)(2,1)} %bitcast.134), kind=kOutput, calls=%fused_computation.25 | convolution fusion | flops 838860800 | bytes 14090240 | tf_op jit(solution)/shard_map/dot_general | solution.py:48
  435.8 5.5 fusion.4
  441.3 2.9 fusion.5
  444.3 5.4 fusion.29
  449.7 0.7 gather_fusion.4
  450.4 83.9 %all-to-all-done.1 = bf16[8,1024,640]{1,2,0:T(8,128)(2,1)} async-done(((bf16[8,1024,640]{1,2,0:T(8,128)(2,1)}), bf16[8,1024,640]{1,2,0:T(8,128)(2,1)}, u32[]{:S(2)}, u32[]{:S(2)}) %all-to-all-start.1) | async-done | bytes 10485792 | tf_op jit(solution)/shard_map/all_to_all | solution.py:103
  534.4 5.7 convolution_bitcast_fusion
  540.3 1.8 copy.59
  542.2 42.1 %reduce-scatter.2.cloned.1.call-done = f32[64,640]{1,0:T(8,128)} async-done(((f32[64,5120]{1,0:T(8,128)}), f32[64,640]{1,0:T(8,128)}) %reduce-scatter.2.cloned.1.call-update) | async-done | bytes 163856 | tf_op jit(solution)/shard_map/reduce_scatter | solution.py:110
  584.3 1.6 convert_element_type.79
  (49 shorter events, 5.4 us)
Async XLA Ops:
  6.5 96.1 %all-gather.3.cloned.1.call-start = ((), (), s32[]{:S(2)}) async-start(), calls=%async_computation.3 | async-start | bytes 13926400 | tf_op jit(solution)/shard_map/all_gather | solution.py:41
  7.3 357.9 %all-gather.5.cloned.1.call-start = ((), (), s32[]{:S(2)}) async-start(), calls=%async_computation.4 | async-start | bytes 11141120 | tf_op jit(solution)/shard_map/all_gather | solution.py:102
  138.1 6.4 %copy-start.1 = (bf16[64,640]{1,0:T(8,128)(2,1)S(1)}, bf16[64,640]{1,0:T(8,128)(2,1)}, u32[]{:S(2)}) copy-start(bf16[64,640]{1,0:T(8,128)(2,1)} %param.7) | copy-start | bytes 245764
  138.1 256.6 %all-to-all-start = ((bf16[640,8,1280]{2,0,1:T(8,128)(2,1)}), bf16[640,8,1280]{2,0,1:T(8,128)(2,1)}, u32[]{:S(2)}, u32[]{:S(2)}) async-start(bf16[640,8,1280]{2,0,1:T(8,128)(2,1)} %copy.52), calls=%async_computation | async-start | bytes 26214400 | tf_op jit(solution)/shard_map/all_to_all | solution.py:42
  394.7 7.4 %copy-start = (s32[64]{0:T(128)S(1)}, s32[64]{0:T(128)}, u32[]{:S(2)}) copy-start(s32[64]{0:T(128)} %param.12) | copy-start | bytes 772
  394.7 7.5 %copy-start.2 = (s32[64]{0:T(128)S(1)}, s32[64]{0:T(128)}, u32[]{:S(2)}) copy-start(s32[64]{0:T(128)} %param.13) | copy-start | bytes 772
  394.7 139.7 %all-to-all-start.1 = ((bf16[8,1024,640]{1,2,0:T(8,128)(2,1)}), bf16[8,1024,640]{1,2,0:T(8,128)(2,1)}, u32[]{:S(2)}, u32[]{:S(2)}) async-start(bf16[8,1024,640]{1,2,0:T(8,128)(2,1)} %copy.57), calls=%async_computation.1 | async-start | bytes 20971520 | tf_op jit(solution)/shard_map/all_to_all | solution.py:103
  401.7 182.5 %reduce-scatter.2.cloned.1.call-start = ((), (), s32[]{:S(2)}) async-start(), calls=%async_computation.5 | async-start | bytes 1474560 | tf_op jit(solution)/shard_map/reduce_scatter | solution.py:110
Sparse Core Ops, SparseCore 0:
  9.8 92.7 all-gather.2
  105.1 210.4 all-gather.4
  542.3 41.8 reduce-scatter.1
where the time goes:
time: 597 us; the launch traced here: 592 us
  waiting for transfers between devices  222 us (37%)
  blocking collectives  220 us (37%)
  local copies, waits for them, and re-layouts  88.6 us (15%)
  matrix products  24.2 us (4%)
  starting transfers between devices  13.5 us (2%)
  between operations  13.3 us (2%)
  other arithmetic  11 us (2%)
    all_gather x1, blocking collectives, local(): full = lax.all_gather(hidden, 'tp', axis=1, tiled=True)  220 us
    all_gather x1, waiting for transfers between devices, local(): grown = lax.all_gather(query_key_value_weight, 'grp', axis=0, tiled=True)  94.7 us
    all_to_all x1, waiting for transfers between devices, local(): lax.all_to_all(grown_out, 'tp', split_axis=0, concat_axis=1, tiled=True)  83.9 us
    reduce_scatter x1, waiting for transfers between devices, local(): lax.psum_scatter(partial_value, 'tp', scatter_dimension=1, tiled=True)  42.1 us
    all_to_all x2, local copies, waits for them, and re-layouts, local(): lax.all_to_all(grown, 'tp', split_axis=1, concat_axis=0, tiled=True)  35.3 us
    all_gather x1, local copies, waits for them, and re-layouts, local(): grown = lax.all_gather(query_key_value_weight, 'grp', axis=0, tiled=True)  17.8 us
    all_to_all x1, local copies, waits for them, and re-layouts, local(): lax.all_to_all(grown_out, 'tp', split_axis=0, concat_axis=1, tiled=True)  15.1 us
    all_gather x1, local copies, waits for them, and re-layouts, local(): grown_out = lax.all_gather(w_out, 'grp', axis=1, tiled=True)  14.4 us
  transfers between devices with their start and end apart: 5, of which 3 were waited for; matrix products, arithmetic and copies ran while one was open for 19% of the time, Pallas kernels for 0%

commit v1 on v0

v1 whole, which is shorter than its diff:
```python
import functools

import jax
import jax.numpy as jnp
import numpy as np
from jax import lax
from jax.experimental import pallas as pl
from jax.experimental.pallas import tpu as pltpu
from jax.sharding import PartitionSpec as P

HEAD_SIZE = 128
PER_KEY = 8
SAMPLES = 8
EPS = 1e-06
ROPE_BASE = 1000000.0
MESH = pl.DeviceIdType.MESH
LOG2E = 1.4426950408889634
MASKED = -1e30
CHUNK = 512

NN = (((1,), (0,)), ((), ()))
NT = (((1,), (1,)), ((), ()))


def dot(a, b, dims=NN):
    return lax.dot_general(a, b, dims, preferred_element_type=jnp.float32)


def layer_kernel(
    size, width, x_ref, w_ref, wo_ref, k_ref, v_ref, len_ref, assign_ref, cos_ref, sin_ref, out_ref,
    xbuf, wbuf, wall, obuf, oall, ssbuf, pbuf, prec, kbuf, vbuf, qs, fresh, lens_sorted, scores, mall, ybuf, yrec,
    local_sem, x_send, x_recv, w_send, w_recv, wf_send, wf_recv, o_send, o_recv, of_send, of_recv,
    ss_send, ss_recv, p_send, p_recv, m_send, m_recv, y_send, y_recv,
):
    g = lax.axis_index("grp")
    t = lax.axis_index("tp")
    q, c = g // 2, g % 2
    rows = x_ref.shape[0]
    head_cols = (PER_KEY + 2) * HEAD_SIZE
    mixed_cols = PER_KEY * HEAD_SIZE
    piece = w_ref.shape[0]
    context = k_ref.shape[1]

    def at(chip, rank):
        return (chip * 2 + c, rank)

    sibling = (q * 2 + 1 - c, t)

    def turn(value, k):
        return lax.rem(value + k, size)

    def remote(src, dst, send, recv, device):
        return pltpu.make_async_remote_copy(
            src_ref=src, dst_ref=dst, send_sem=send, recv_sem=recv, device_id=device, device_id_type=MESH
        )

    k_copy = pltpu.make_async_copy(k_ref, kbuf, local_sem.at[0])
    v_copy = pltpu.make_async_copy(v_ref, vbuf, local_sem.at[1])

    barrier = pltpu.get_barrier_semaphore()

    def greet(device):
        pl.semaphore_signal(barrier, inc=1, device_id=device, device_id_type=MESH)

    greet(sibling)
    for k in range(1, size):
        greet((g, turn(t, k)))
        greet(at(turn(q, k), t))
        greet(at(t, turn(t, k)))
        greet(at(turn(q, k), q))

    @pl.when(q != t)
    def _():
        greet(at(t, t))
        greet(at(q, q))

    pl.semaphore_wait(barrier, jnp.where(q == t, 4 * size - 3, 4 * size - 1))

    def x_copy(k):
        return remote(x_ref, xbuf.at[q], x_send.at[k], x_recv.at[q], at(t, turn(t, k)))

    own_x = pltpu.make_async_copy(x_ref, xbuf.at[q], x_recv.at[q])

    def w_copy(k):
        rank = turn(t, k)
        cols = pl.ds(pl.multiple_of(rank * head_cols, HEAD_SIZE), head_cols)
        return remote(w_ref.at[:, cols], wbuf.at[c, t], w_send.at[k], w_recv.at[t], (g, rank))

    own_cols = pl.ds(pl.multiple_of(t * head_cols, HEAD_SIZE), head_cols)
    own_w = pltpu.make_async_copy(w_ref.at[:, own_cols], wbuf.at[c, t], w_recv.at[t])

    def o_copy(k):
        rank = turn(t, k)
        cols = pl.ds(pl.multiple_of(rank * mixed_cols, HEAD_SIZE), mixed_cols)
        return remote(wo_ref.at[:, cols], obuf.at[c, t], o_send.at[k], o_recv.at[t], (g, rank))

    own_mixed = pl.ds(pl.multiple_of(t * mixed_cols, HEAD_SIZE), mixed_cols)
    own_o = pltpu.make_async_copy(wo_ref.at[:, own_mixed], obuf.at[c, t], o_recv.at[t])

    own_w.start()
    for k in range(1, size):
        w_copy(k).start()

    @pl.when(q == t)
    def _():
        own_x.start()

    @pl.when(q != t)
    def _():
        x_copy(0).start()

    for k in range(1, size):
        x_copy(k).start()
    own_o.start()
    for k in range(1, size):
        o_copy(k).start()
    k_copy.start()
    v_copy.start()

    x32 = x_ref[...].astype(jnp.float32)
    squares = jnp.sum(x32 * x32, axis=-1, keepdims=True)
    lane_row = lax.broadcasted_iota(jnp.int32, (rows, HEAD_SIZE), 0)
    lane_col = lax.broadcasted_iota(jnp.int32, (rows, HEAD_SIZE), 1)
    as_row = jnp.sum(jnp.where(lane_row == lane_col, squares, 0.0), axis=0, keepdims=True)
    ssbuf[t] = jnp.broadcast_to(as_row, (8, HEAD_SIZE))

    def ss_copy(k):
        return remote(ssbuf.at[t], ssbuf.at[t], ss_send.at[k], ss_recv.at[t], (g, turn(t, k)))

    for k in range(1, size):
        ss_copy(k).start()

    assign_row = jnp.broadcast_to(assign_ref[...], (rows, rows))
    i_row = lax.broadcasted_iota(jnp.int32, (rows, rows), 0)
    i_col = lax.broadcasted_iota(jnp.int32, (rows, rows), 1)
    diagonal = i_row == i_col

    def column(row_values):
        return jnp.sum(jnp.where(diagonal, row_values, 0.0), axis=1, keepdims=True)

    assign_f = assign_row.astype(jnp.float32)
    same = assign_f == column(assign_f)
    earlier = jnp.sum(jnp.where(same, jnp.where(i_row < i_col, 1.0, 0.0), 0.0), axis=0, keepdims=True)
    place_row = assign_f * SAMPLES + earlier
    place_col = column(place_row)
    sort_mat = jnp.where(i_row.astype(jnp.float32) == place_row, 1.0, 0.0)
    back_mat = jnp.where(i_col.astype(jnp.float32) == place_col, 1.0, 0.0).astype(jnp.bfloat16)
    len_row = len_ref[...].astype(jnp.float32)
    lens_sorted[...] = jnp.broadcast_to(
        jnp.sum(sort_mat * len_row, axis=1, keepdims=True), (rows, HEAD_SIZE)
    )
    sort_mat = sort_mat.astype(jnp.bfloat16)

    def wf_copy(s):
        return remote(wbuf.at[c, s], wbuf.at[c, s], wf_send.at[s], wf_recv.at[s], sibling)

    def of_copy(s):
        return remote(obuf.at[c, s], obuf.at[c, s], of_send.at[s], of_recv.at[s], sibling)

    def await_into(ref, sem):
        pltpu.make_async_copy(ref, ref, sem).wait()

    for s in range(size):
        await_into(wbuf.at[c, s], w_recv.at[s])
        wf_copy(s).start()
    for s in range(size):
        await_into(wbuf.at[1 - c, s], wf_recv.at[s])
    for core in range(2):
        for s in range(size):
            first = (core * size + s) * piece
            wall[first : first + piece, :] = wbuf[core, s]

    def p_copy(k):
        return remote(pbuf.at[k], prec.at[q], p_send.at[k], p_recv.at[q], at(turn(q, k), t))

    def project(k):
        chip = turn(q, k)
        await_into(xbuf.at[chip], x_recv.at[chip])
        return dot(xbuf[chip], wall[...])

    def project_step(k, carry):
        pbuf[k] = project(k)
        p_copy(k).start()
        return carry

    lax.fori_loop(1, size, project_step, 0)
    prec[q] = project(0)

    for s in range(size):
        await_into(obuf.at[c, s], o_recv.at[s])
        of_copy(s).start()
    for s in range(size):
        await_into(obuf.at[1 - c, s], of_recv.at[s])
    for core in range(2):
        for s in range(size):
            first = (core * size + s) * piece
            oall[first : first + piece, :] = obuf[core, s]

    for k in range(1, size):
        rank = turn(t, k)
        await_into(ssbuf.at[rank], ss_recv.at[rank])
    total_row = ssbuf[0]
    for s in range(1, size):
        total_row = total_row + ssbuf[s]
    total = jnp.sum(jnp.where(lane_row == lane_col, total_row[:1], 0.0), axis=1, keepdims=True)
    row_scale = lax.rsqrt(total * (1.0 / width) + EPS)

    for k in range(1, size):
        chip = turn(q, k)
        await_into(prec.at[chip], p_recv.at[chip])

    cosine, sine = cos_ref[...], sin_ref[...]
    for h in range(PER_KEY + 2):
        cols = slice(h * HEAD_SIZE, (h + 1) * HEAD_SIZE)
        head = prec[0, :, cols]
        for s in range(1, size):
            head = head + prec[s, :, cols]
        head = head * row_scale
        if h <= PER_KEY:
            head = head * lax.rsqrt(jnp.mean(head * head, axis=-1, keepdims=True) + EPS)
            head = head * cosine + pltpu.roll(head, HEAD_SIZE // 2, 1) * sine
        ordered = dot(sort_mat, head.astype(jnp.bfloat16))
        if h < PER_KEY:
            qs[h] = ordered
        else:
            fresh[h - PER_KEY] = ordered

    k_copy.wait()
    v_copy.wait()
    scale2 = HEAD_SIZE ** (-0.5) * LOG2E
    queries = PER_KEY * SAMPLES
    slot_iota = lax.broadcasted_iota(jnp.int32, (queries, HEAD_SIZE), 1).astype(jnp.float32)

    def attend(p):
        mine = pl.ds(pl.multiple_of(p * SAMPLES, SAMPLES), SAMPLES)
        query = qs[:, mine, :]
        own = jnp.sum(query * fresh[0, mine, :][None], axis=-1, keepdims=True).reshape(queries, 1)
        fresh_value = jnp.broadcast_to(fresh[1, mine, :][None], query.shape).reshape(queries, HEAD_SIZE)
        seen = jnp.broadcast_to(lens_sorted[mine, :][None], query.shape).reshape(queries, HEAD_SIZE)
        query = query.reshape(queries, HEAD_SIZE).astype(jnp.bfloat16)
        top = jnp.full((queries, HEAD_SIZE), MASKED, jnp.float32)
        for chunk in range(context // CHUNK):
            part = dot(query, kbuf[p, chunk * CHUNK : (chunk + 1) * CHUNK, :], NT)
            for lane in range(CHUNK // HEAD_SIZE):
                first = chunk * CHUNK + lane * HEAD_SIZE
                tile = part[:, lane * HEAD_SIZE : (lane + 1) * HEAD_SIZE]
                tile = jnp.where(slot_iota < seen - first, tile, MASKED)
                scores[:, first : first + HEAD_SIZE] = tile
                top = jnp.maximum(top, tile)
        peak = jnp.maximum(jnp.max(top, axis=-1, keepdims=True), own)
        shift = peak * scale2
        own_weight = jnp.exp2(own * scale2 - shift)
        sums = jnp.zeros((queries, HEAD_SIZE), jnp.float32)
        mixed = own_weight * fresh_value
        for chunk in range(context // CHUNK):
            cols = slice(chunk * CHUNK, (chunk + 1) * CHUNK)
            weights = jnp.exp2(scores[:, cols] * scale2 - shift)
            for lane in range(CHUNK // HEAD_SIZE):
                sums = sums + weights[:, lane * HEAD_SIZE : (lane + 1) * HEAD_SIZE]
            mixed = mixed + dot(weights.astype(jnp.bfloat16), vbuf[p, cols, :])
        return mixed / (jnp.sum(sums, axis=-1, keepdims=True) + own_weight)

    def m_copy(i, k):
        return remote(mall.at[q, i], mall.at[q, i], m_send.at[i, k], m_recv.at[i, q], at(turn(q, k), t))

    def attend_pair(i, carry):
        low, high = attend(2 * i), attend(2 * i + 1)
        for h in range(PER_KEY):
            part = slice(h * SAMPLES, (h + 1) * SAMPLES)
            mall[q, i, :, h * HEAD_SIZE : (h + 1) * HEAD_SIZE] = jnp.concatenate(
                [low[part], high[part]], axis=0
            ).astype(jnp.bfloat16)
        for k in range(1, size):
            m_copy(i, k).start()
        return carry

    pairs = kbuf.shape[0] // 2
    lax.fori_loop(0, pairs, attend_pair, 0)

    def y_copy(k):
        return remote(ybuf.at[k], yrec.at[t], y_send.at[k], y_recv.at[t], at(turn(q, k), q))

    own_y = pltpu.make_async_copy(ybuf.at[0], yrec.at[t], y_recv.at[t])

    def out_block(k):
        chip = turn(q, k)
        ybuf[k] = dot(mall[chip].reshape(rows, mixed_cols), oall[...], NT)

    out_block(0)

    @pl.when(q == t)
    def _():
        own_y.start()

    @pl.when(q != t)
    def _():
        y_copy(0).start()

    def out_step(k, carry):
        chip = turn(q, k)
        for i in range(pairs):
            await_into(mall.at[chip, i], m_recv.at[i, chip])
        out_block(k)
        y_copy(k).start()
        return carry

    lax.fori_loop(1, size, out_step, 0)

    for s in range(size):
        await_into(yrec.at[s], y_recv.at[s])
    result = yrec[0]
    for s in range(1, size):
        result = result + yrec[s]
    out_ref[...] = dot(back_mat, result.astype(jnp.bfloat16)).astype(jnp.bfloat16)

    @pl.when(q != t)
    def _():
        x_copy(0).wait_send()
        y_copy(0).wait_send()

    for k in range(1, size):
        x_copy(k).wait_send()
        w_copy(k).wait_send()
        o_copy(k).wait_send()
        ss_copy(k).wait_send()
        p_copy(k).wait_send()
        y_copy(k).wait_send()
        for i in range(pairs):
            m_copy(i, k).wait_send()
    for s in range(size):
        wf_copy(s).wait_send()
        of_copy(s).wait_send()


def local(size, hidden, query_key_value_weight, w_out, k_cache, value_cache, lengths, assign):
    rows, features = hidden.shape
    width = features * size
    piece = query_key_value_weight.shape[0]
    prompts, context = k_cache.shape[0], k_cache.shape[1]
    half = HEAD_SIZE // 2
    freq = ROPE_BASE ** (-jnp.arange(half, dtype=jnp.float32) * 2.0 / HEAD_SIZE)
    angle = lengths.astype(jnp.float32)[:, None] * freq[None, :]
    cosine, sine = jnp.cos(angle), jnp.sin(angle)
    cosine = jnp.concatenate([cosine, cosine], axis=1)
    sine = jnp.concatenate([-sine, sine], axis=1)
    head_cols = (PER_KEY + 2) * HEAD_SIZE
    mixed_cols = PER_KEY * HEAD_SIZE
    bf16, f32 = jnp.bfloat16, jnp.float32
    dma = pltpu.SemaphoreType.DMA
    pairs = prompts // 2
    vmem = pl.BlockSpec(memory_space=pltpu.VMEM)
    anywhere = pl.BlockSpec(memory_space=pl.ANY)
    return pl.pallas_call(
        functools.partial(layer_kernel, size, width),
        out_shape=jax.ShapeDtypeStruct((rows, features), bf16),
        in_specs=[vmem, anywhere, anywhere, anywhere, anywhere, vmem, vmem, vmem, vmem],
        out_specs=vmem,
        scratch_shapes=[
            pltpu.VMEM((size, rows, features), bf16),
            pltpu.VMEM((2, size, piece, head_cols), bf16),
            pltpu.VMEM((features, head_cols), bf16),
            pltpu.VMEM((2, size, piece, mixed_cols), bf16),
            pltpu.VMEM((features, mixed_cols), bf16),
            pltpu.VMEM((size, 8, HEAD_SIZE), f32),
            pltpu.VMEM((size, rows, head_cols), f32),
            pltpu.VMEM((size, rows, head_cols), f32),
            pltpu.VMEM((prompts, context, HEAD_SIZE), bf16),
            pltpu.VMEM((prompts, context, HEAD_SIZE), bf16),
            pltpu.VMEM((PER_KEY, rows, HEAD_SIZE), f32),
            pltpu.VMEM((2, rows, HEAD_SIZE), f32),
            pltpu.VMEM((rows, HEAD_SIZE), f32),
            pltpu.VMEM((PER_KEY * SAMPLES, context), f32),
            pltpu.VMEM((size, pairs, 2 * SAMPLES, mixed_cols), bf16),
            pltpu.VMEM((size, rows, features), f32),
            pltpu.VMEM((size, rows, features), f32),
            dma((2,)),
            dma((size,)), dma((size,)),
            dma((size,)), dma((size,)), dma((size,)), dma((size,)),
            dma((size,)), dma((size,)), dma((size,)), dma((size,)),
            dma((size,)), dma((size,)),
            dma((size,)), dma((size,)),
            dma((pairs, size)), dma((pairs, size)),
            dma((size,)), dma((size,)),
        ],
        compiler_params=pltpu.CompilerParams(
            collective_id=0, has_side_effects=True, vmem_limit_bytes=56 * 1024 * 1024
        ),
        name="layer",
    )(
        hidden,
        query_key_value_weight,
        w_out.T,
        k_cache.reshape(prompts, context, HEAD_SIZE),
        value_cache.reshape(prompts, context, HEAD_SIZE),
        lengths.reshape(1, rows),
        assign.reshape(1, rows),
        cosine,
        sine,
    )


def solution(mesh):
    return jax.shard_map(
        functools.partial(local, mesh.shape["tp"]),
        mesh=mesh,
        in_specs=(
            P("grp", "tp"),
            P(("grp", "tp"), None),
            P(None, ("grp", "tp")),
            P("grp", None, "tp", None),
            P("grp", None, "tp", None),
            P("grp"),
            P("grp"),
        ),
        out_specs=P("grp", "tp"),
        check_vma=False,
    )
```

time: 597 us -> 204 us (0.34)
  the two profiles are of different devices: /device:TPU:20 before, /device:TPU:104 now
where the time goes in v1:
time: 204 us
  Pallas kernels  201 us (99%)
    pallas_call x1, Pallas kernels, local(): pl.pallas_call(functools.partial(layer_kernel, size, width), out_shape=ja...  201 us

profile of v1, /device:TPU:104, one launch (start us, length us, event | category | flops | bytes accessed | tf_op | source)
XLA Modules:
  0.0 204.1 jit_solution(9406443038999286160)
XLA Ops:
  0.0 0.7 convert_element_type.3
  0.7 0.2 fusion
  0.9 0.7 pad_maximum_fusion
  1.6 201.0 %layer.1 = bf16[64,640]{1,0:T(8,128)(2,1)} custom-call(bf16[64,640]{1,0:T(8,128)(2,1)} %x_ref.1, bf16[40,10240]{1,0:T(8,128)(2,1)} %w_ref.1, bf16[40,8192]{1,0:T(8,128)(2,1)} %bitcast.7, bf16[8,4096,128]{2,1,0:T(8,128)(2,1)} %bitcast.5, bf16[8,4096,128]{2,1,0:T(8,128)(2,1)} %bitcast.6, s32[1,64]{1,0:T(1,128)} %bitcast.8, s32[1,64]{1,0:T(1,128)} %bitcast.9, ...), custom_call_target="tpu_custom_call" | custom-call | tf_op jit(solution)/shard_map/layer/pallas_call | solution.py:353
  202.6 1.5 copy.9
  (1 shorter events, 0.0 us)

commit v2 on v1

v2 whole, which is shorter than its diff:
```python
import functools

import jax
import jax.numpy as jnp
import numpy as np
from jax import lax
from jax.experimental import pallas as pl
from jax.experimental.pallas import tpu as pltpu
from jax.sharding import PartitionSpec as P

HEAD_SIZE = 128
PER_KEY = 8
SAMPLES = 8
EPS = 1e-06
ROPE_BASE = 1000000.0
MESH = pl.DeviceIdType.MESH
LOG2E = 1.4426950408889634
MASKED = -1e30
CHUNK = 512
P_TYPE = jnp.bfloat16
Y_TYPE = jnp.bfloat16

NN = (((1,), (0,)), ((), ()))
NT = (((1,), (1,)), ((), ()))


def dot(a, b, dims=NN):
    return lax.dot_general(a, b, dims, preferred_element_type=jnp.float32)


def layer_kernel(
    size, width, x_ref, w_ref, wo_ref, k_ref, v_ref, len_ref, assign_ref, freq_ref, out_ref,
    xgot, xsend, xbuf, wbuf, wall, obuf, oall, pbuf, prec, pown, kbuf, vbuf, qs, fresh, lens_sorted, scores,
    mall, ybuf, yrec, yown, zbuf, zrec,
    local_sem, g_send, g_recv, x_send, x_recv, w_send, w_recv, wf_send, wf_recv, o_send, o_recv, of_send, of_recv,
    p_send, p_recv, m_send, m_recv, y_send, y_recv, z_send, z_recv,
):
    g = lax.axis_index("grp")
    t = lax.axis_index("tp")
    q, c = g // 2, g % 2
    rows = x_ref.shape[0]
    head_cols = (PER_KEY + 2) * HEAD_SIZE
    mixed_cols = PER_KEY * HEAD_SIZE
    piece = w_ref.shape[0]
    context = k_ref.shape[1]
    pairs = k_ref.shape[0] // 2

    sibling = (q * 2 + 1 - c, t)
    mirror = (t * 2 + c, q)

    def turn(value, k):
        return lax.rem(value + k, size)

    def rank_peer(k):
        return (g, turn(t, k))

    def chip_peer(k):
        return (turn(q, k) * 2 + c, t)

    def remote(src, dst, send, recv, device):
        return pltpu.make_async_remote_copy(
            src_ref=src, dst_ref=dst, send_sem=send, recv_sem=recv, device_id=device, device_id_type=MESH
        )

    def await_into(ref, sem):
        pltpu.make_async_copy(ref, ref, sem).wait()

    barrier = pltpu.get_barrier_semaphore()

    def greet(device):
        pl.semaphore_signal(barrier, inc=1, device_id=device, device_id_type=MESH)

    for k in range(1, size):
        greet(rank_peer(k))
        greet(chip_peer(k))
    greet(sibling)

    @pl.when(q != t)
    def _():
        greet(mirror)

    k_copy = pltpu.make_async_copy(k_ref, kbuf, local_sem.at[0])
    v_copy = pltpu.make_async_copy(v_ref, vbuf, local_sem.at[1])
    k_copy.start()
    v_copy.start()

    assign_row = jnp.broadcast_to(assign_ref[...], (rows, rows))
    i_row = lax.broadcasted_iota(jnp.int32, (rows, rows), 0)
    i_col = lax.broadcasted_iota(jnp.int32, (rows, rows), 1)
    diagonal = i_row == i_col

    def column(row_values):
        return jnp.sum(jnp.where(diagonal, row_values, 0.0), axis=1, keepdims=True)

    assign_f = assign_row.astype(jnp.float32)
    same = assign_f == column(assign_f)
    earlier = jnp.sum(jnp.where(same, jnp.where(i_row < i_col, 1.0, 0.0), 0.0), axis=0, keepdims=True)
    place_row = assign_f * SAMPLES + earlier
    place_col = column(place_row)
    sort_mat = jnp.where(i_row.astype(jnp.float32) == place_row, 1.0, 0.0)
    back_mat = jnp.where(i_col.astype(jnp.float32) == place_col, 1.0, 0.0).astype(jnp.bfloat16)
    lens = jnp.sum(sort_mat * len_ref[...].astype(jnp.float32), axis=1, keepdims=True)
    lens_sorted[...] = jnp.broadcast_to(lens, (rows, HEAD_SIZE))
    xgot[t] = dot(sort_mat.astype(jnp.bfloat16), x_ref[...]).astype(jnp.bfloat16)

    pl.semaphore_wait(barrier, jnp.where(q == t, 2 * size - 1, 2 * size))

    def g_copy(k):
        return remote(xgot.at[t], xgot.at[t], g_send.at[k], g_recv.at[t], rank_peer(k))

    def w_copy(k):
        cols = pl.ds(pl.multiple_of(turn(t, k) * head_cols, HEAD_SIZE), head_cols)
        return remote(w_ref.at[:, cols], wbuf.at[c, t], w_send.at[k], w_recv.at[t], rank_peer(k))

    def o_copy(k):
        cols = pl.ds(pl.multiple_of(turn(t, k) * mixed_cols, HEAD_SIZE), mixed_cols)
        return remote(wo_ref.at[:, cols], obuf.at[c, t], o_send.at[k], o_recv.at[t], rank_peer(k))

    own_cols = pl.ds(pl.multiple_of(t * head_cols, HEAD_SIZE), head_cols)
    own_w = pltpu.make_async_copy(w_ref.at[:, own_cols], wbuf.at[c, t], w_recv.at[t])
    own_mixed = pl.ds(pl.multiple_of(t * mixed_cols, HEAD_SIZE), mixed_cols)
    own_o = pltpu.make_async_copy(wo_ref.at[:, own_mixed], obuf.at[c, t], o_recv.at[t])

    for k in range(1, size):
        g_copy(k).start()
    own_w.start()
    own_o.start()
    for k in range(1, size):
        w_copy(k).start()

    angle = lens * freq_ref[...]
    lane = lax.broadcasted_iota(jnp.int32, (rows, HEAD_SIZE), 1)
    cosine = jnp.cos(angle)
    sine = jnp.where(lane < HEAD_SIZE // 2, -1.0, 1.0) * jnp.sin(angle)

    for k in range(1, size):
        await_into(xgot.at[turn(t, k)], g_recv.at[turn(t, k)])
    squares = jnp.zeros((rows, 1), jnp.float32)
    for s in range(size):
        features = xgot[s].astype(jnp.float32)
        squares = squares + jnp.sum(features * features, axis=-1, keepdims=True)
    row_scale = lax.rsqrt(squares * (1.0 / width) + EPS)

    def x_copy(k):
        return remote(xsend.at[turn(q, k)], xbuf.at[q], x_send.at[k], x_recv.at[q], chip_peer(k))

    for k in range(1, size):
        chip = turn(q, k)
        xsend[chip] = (xgot[chip].astype(jnp.float32) * row_scale).astype(jnp.bfloat16)
        x_copy(k).start()
    xsend[q] = (xgot[q].astype(jnp.float32) * row_scale).astype(jnp.bfloat16)

    def wf_copy(s):
        return remote(wbuf.at[c, s], wbuf.at[c, s], wf_send.at[s], wf_recv.at[s], sibling)

    def of_copy(s):
        return remote(obuf.at[c, s], obuf.at[c, s], of_send.at[s], of_recv.at[s], sibling)

    for s in range(size):
        await_into(wbuf.at[c, s], w_recv.at[s])
        wf_copy(s).start()
    for k in range(1, size):
        o_copy(k).start()
    for s in range(size):
        await_into(wbuf.at[1 - c, s], wf_recv.at[s])
    for core in range(2):
        for s in range(size):
            first = (core * size + s) * piece
            wall[first : first + piece, :] = wbuf[core, s]

    def p_copy(k):
        return remote(pbuf.at[k], prec.at[q], p_send.at[k], p_recv.at[q], chip_peer(k))

    def project_step(k, carry):
        chip = turn(q, k)
        await_into(xbuf.at[chip], x_recv.at[chip])
        pbuf[k] = dot(xbuf[chip], wall[...]).astype(pbuf.dtype)
        p_copy(k).start()
        return carry

    lax.fori_loop(1, size, project_step, 0)
    pown[...] = dot(xsend[q], wall[...])

    for s in range(size):
        await_into(obuf.at[c, s], o_recv.at[s])
        of_copy(s).start()
    for s in range(size):
        await_into(obuf.at[1 - c, s], of_recv.at[s])
    for core in range(2):
        for s in range(size):
            first = (core * size + s) * piece
            oall[first : first + piece, :] = obuf[core, s]

    for k in range(1, size):
        await_into(prec.at[turn(q, k)], p_recv.at[turn(q, k)])

    for h in range(PER_KEY + 2):
        cols = slice(h * HEAD_SIZE, (h + 1) * HEAD_SIZE)
        head = pown[:, cols]
        for k in range(1, size):
            head = head + prec[turn(q, k), :, cols].astype(jnp.float32)
        if h <= PER_KEY:
            head = head * lax.rsqrt(jnp.mean(head * head, axis=-1, keepdims=True) + EPS)
            head = head * cosine + pltpu.roll(head, HEAD_SIZE // 2, 1) * sine
        head = head.astype(jnp.bfloat16).astype(jnp.float32)
        if h < PER_KEY:
            qs[h] = head
        else:
            fresh[h - PER_KEY] = head

    k_copy.wait()
    v_copy.wait()
    scale2 = HEAD_SIZE ** (-0.5) * LOG2E
    queries = PER_KEY * SAMPLES
    slot_iota = lax.broadcasted_iota(jnp.int32, (queries, HEAD_SIZE), 1).astype(jnp.float32)

    def attend(p):
        mine = pl.ds(pl.multiple_of(p * SAMPLES, SAMPLES), SAMPLES)
        query = qs[:, mine, :]
        own = jnp.sum(query * fresh[0, mine, :][None], axis=-1, keepdims=True).reshape(queries, 1)
        fresh_value = jnp.broadcast_to(fresh[1, mine, :][None], query.shape).reshape(queries, HEAD_SIZE)
        seen = jnp.broadcast_to(lens_sorted[mine, :][None], query.shape).reshape(queries, HEAD_SIZE)
        query = query.reshape(queries, HEAD_SIZE).astype(jnp.bfloat16)
        top = jnp.full((queries, HEAD_SIZE), MASKED, jnp.float32)
        for chunk in range(context // CHUNK):
            part = dot(query, kbuf[p, chunk * CHUNK : (chunk + 1) * CHUNK, :], NT)
            for lane in range(CHUNK // HEAD_SIZE):
                first = chunk * CHUNK + lane * HEAD_SIZE
                tile = part[:, lane * HEAD_SIZE : (lane + 1) * HEAD_SIZE]
                tile = jnp.where(slot_iota < seen - first, tile, MASKED)
                scores[:, first : first + HEAD_SIZE] = tile
                top = jnp.maximum(top, tile)
        peak = jnp.maximum(jnp.max(top, axis=-1, keepdims=True), own)
        shift = peak * scale2
        own_weight = jnp.exp2(own * scale2 - shift)
        sums = jnp.zeros((queries, HEAD_SIZE), jnp.float32)
        for chunk in range(context // CHUNK):
            cols = slice(chunk * CHUNK, (chunk + 1) * CHUNK)
            weights = jnp.exp2(scores[:, cols] * scale2 - shift)
            scores[:, cols] = weights
            for lane in range(CHUNK // HEAD_SIZE):
                sums = sums + weights[:, lane * HEAD_SIZE : (lane + 1) * HEAD_SIZE]
        part = 1.0 / (jnp.sum(sums, axis=-1, keepdims=True) + own_weight)
        mixed = (own_weight * part).astype(jnp.bfloat16).astype(jnp.float32) * fresh_value
        for chunk in range(context // CHUNK):
            cols = slice(chunk * CHUNK, (chunk + 1) * CHUNK)
            mixed = mixed + dot((scores[:, cols] * part).astype(jnp.bfloat16), vbuf[p, cols, :])
        return mixed

    def m_copy(i, k):
        return remote(mall.at[q, i], mall.at[q, i], m_send.at[i, k], m_recv.at[i, q], chip_peer(k))

    def attend_pair(i, carry):
        low, high = attend(2 * i), attend(2 * i + 1)
        for h in range(PER_KEY):
            part = slice(h * SAMPLES, (h + 1) * SAMPLES)
            mall[q, i, :, h * HEAD_SIZE : (h + 1) * HEAD_SIZE] = jnp.concatenate(
                [low[part], high[part]], axis=0
            ).astype(jnp.bfloat16)
        for k in range(1, size):
            m_copy(i, k).start()
        return carry

    lax.fori_loop(0, pairs, attend_pair, 0)

    def y_copy(k):
        return remote(ybuf.at[k], yrec.at[t], y_send.at[k], y_recv.at[t], rank_peer(k))

    def out_step(k, carry):
        chip = turn(t, k)

        @pl.when(chip != q)
        def _():
            for i in range(pairs):
                await_into(mall.at[chip, i], m_recv.at[i, chip])

        ybuf[k] = dot(mall[chip].reshape(rows, mixed_cols), oall[...], NT).astype(ybuf.dtype)
        y_copy(k).start()
        return carry

    lax.fori_loop(1, size, out_step, 0)

    @pl.when(t != q)
    def _():
        for i in range(pairs):
            await_into(mall.at[t, i], m_recv.at[i, t])

    yown[...] = dot(mall[t].reshape(rows, mixed_cols), oall[...], NT)
    for k in range(1, size):
        await_into(yrec.at[turn(t, k)], y_recv.at[turn(t, k)])
    result = yown[...]
    for k in range(1, size):
        result = result + yrec[turn(t, k)].astype(jnp.float32)
    zbuf[...] = result.astype(jnp.bfloat16)

    z_copy = remote(zbuf, zrec, z_send, z_recv, mirror)

    @pl.when(q != t)
    def _():
        z_copy.start()
        z_copy.wait()

    @pl.when(q == t)
    def _():
        zrec[...] = zbuf[...]

    out_ref[...] = dot(back_mat, zrec[...]).astype(jnp.bfloat16)

    for k in range(1, size):
        g_copy(k).wait_send()
        x_copy(k).wait_send()
        w_copy(k).wait_send()
        o_copy(k).wait_send()
        p_copy(k).wait_send()
        y_copy(k).wait_send()
        for i in range(pairs):
            m_copy(i, k).wait_send()
    for s in range(size):
        wf_copy(s).wait_send()
        of_copy(s).wait_send()


def local(size, hidden, query_key_value_weight, w_out, k_cache, value_cache, lengths, assign):
    rows, features = hidden.shape
    width = features * size
    piece = query_key_value_weight.shape[0]
    prompts, context = k_cache.shape[0], k_cache.shape[1]
    half = np.arange(HEAD_SIZE // 2, dtype=np.float32)
    freq = np.float32(ROPE_BASE) ** (-half * np.float32(2.0) / np.float32(HEAD_SIZE))
    freq = np.concatenate([freq, freq]).astype(np.float32)[None, :]
    head_cols = (PER_KEY + 2) * HEAD_SIZE
    mixed_cols = PER_KEY * HEAD_SIZE
    bf16, f32 = jnp.bfloat16, jnp.float32
    dma = pltpu.SemaphoreType.DMA
    pairs = prompts // 2
    vmem = pl.BlockSpec(memory_space=pltpu.VMEM)
    anywhere = pl.BlockSpec(memory_space=pl.ANY)
    return pl.pallas_call(
        functools.partial(layer_kernel, size, width),
        out_shape=jax.ShapeDtypeStruct((rows, features), bf16),
        in_specs=[vmem, anywhere, anywhere, anywhere, anywhere, vmem, vmem, vmem],
        out_specs=vmem,
        scratch_shapes=[
            pltpu.VMEM((size, rows, features), bf16),
            pltpu.VMEM((size, rows, features), bf16),
            pltpu.VMEM((size, rows, features), bf16),
            pltpu.VMEM((2, size, piece, head_cols), bf16),
            pltpu.VMEM((features, head_cols), bf16),
            pltpu.VMEM((2, size, piece, mixed_cols), bf16),
            pltpu.VMEM((features, mixed_cols), bf16),
            pltpu.VMEM((size, rows, head_cols), P_TYPE),
            pltpu.VMEM((size, rows, head_cols), P_TYPE),
            pltpu.VMEM((rows, head_cols), f32),
            pltpu.VMEM((prompts, context, HEAD_SIZE), bf16),
            pltpu.VMEM((prompts, context, HEAD_SIZE), bf16),
            pltpu.VMEM((PER_KEY, rows, HEAD_SIZE), f32),
            pltpu.VMEM((2, rows, HEAD_SIZE), f32),
            pltpu.VMEM((rows, HEAD_SIZE), f32),
            pltpu.VMEM((PER_KEY * SAMPLES, context), f32),
            pltpu.VMEM((size, pairs, 2 * SAMPLES, mixed_cols), bf16),
            pltpu.VMEM((size, rows, features), Y_TYPE),
            pltpu.VMEM((size, rows, features), Y_TYPE),
            pltpu.VMEM((rows, features), f32),
            pltpu.VMEM((rows, features), bf16),
            pltpu.VMEM((rows, features), bf16),
            dma((2,)),
            dma((size,)), dma((size,)),
            dma((size,)), dma((size,)),
            dma((size,)), dma((size,)), dma((size,)), dma((size,)),
            dma((size,)), dma((size,)), dma((size,)), dma((size,)),
            dma((size,)), dma((size,)),
            dma((pairs, size)), dma((pairs, size)),
            dma((size,)), dma((size,)),
            dma, dma,
        ],
        compiler_params=pltpu.CompilerParams(
            collective_id=0, has_side_effects=True, vmem_limit_bytes=56 * 1024 * 1024
        ),
        name="layer",
    )(
        hidden,
        query_key_value_weight,
        w_out.T,
        k_cache.reshape(prompts, context, HEAD_SIZE),
        value_cache.reshape(prompts, context, HEAD_SIZE),
        lengths.reshape(1, rows),
        assign.reshape(1, rows),
        jnp.asarray(freq),
    )


def solution(mesh):
    return jax.shard_map(
        functools.partial(local, mesh.shape["tp"]),
        mesh=mesh,
        in_specs=(
            P("grp", "tp"),
            P(("grp", "tp"), None),
            P(None, ("grp", "tp")),
            P("grp", None, "tp", None),
            P("grp", None, "tp", None),
            P("grp"),
            P("grp"),
        ),
        out_specs=P("grp", "tp"),
        check_vma=False,
    )
```

time: 204 us -> 95.7 us (0.47)
  the two profiles are of different devices: /device:TPU:104 before, /device:TPU:6 now
where the time goes in v2:
time: 95.7 us; the launch traced here: 95.5 us
  Pallas kernels  94 us (98%)
  local copies, waits for them, and re-layouts  1.53 us (2%)
    pallas_call x1, Pallas kernels, local(): pl.pallas_call(functools.partial(layer_kernel, size, width), out_shape=ja...  94 us

profile of v2, /device:TPU:6, one launch (start us, length us, event | category | flops | bytes accessed | tf_op | source)
XLA Modules:
  0.0 95.5 jit_solution(11717193308131870994)
XLA Ops:
  0.0 94.0 %layer.1 = bf16[64,640]{1,0:T(8,128)(2,1)} custom-call(bf16[64,640]{1,0:T(8,128)(2,1)} %x_ref.1, bf16[40,10240]{1,0:T(8,128)(2,1)} %w_ref.1, bf16[40,8192]{1,0:T(8,128)(2,1)} %bitcast.7, bf16[8,4096,128]{2,1,0:T(8,128)(2,1)} %bitcast.5, bf16[8,4096,128]{2,1,0:T(8,128)(2,1)} %bitcast.6, s32[1,64]{1,0:T(1,128)} %bitcast.8, s32[1,64]{1,0:T(1,128)} %bitcast.9, ...), custom_call_target="tpu_custom_call" | custom-call | tf_op jit(solution)/shard_map/layer/pallas_call | solution.py:338
  94.0 1.5 %copy.10 = bf16[64,640]{1,0:T(8,128)(2,1)} copy(bf16[64,640]{1,0:T(8,128)(2,1)} %layer.1) | data formatting | bytes 163840

commit v3 on v2

v3 whole, which is shorter than its diff:
```python
import functools

import jax
import jax.numpy as jnp
import numpy as np
from jax import lax
from jax.experimental import pallas as pl
from jax.experimental.pallas import tpu as pltpu
from jax.sharding import PartitionSpec as P

HEAD_SIZE = 128
PER_KEY = 8
SAMPLES = 8
EPS = 1e-06
ROPE_BASE = 1000000.0
MESH = pl.DeviceIdType.MESH
LOG2E = 1.4426950408889634
MASKED = -1e30
CHUNK = 512
P_TYPE = jnp.bfloat16
Y_TYPE = jnp.bfloat16

NN = (((1,), (0,)), ((), ()))
NT = (((1,), (1,)), ((), ()))


def dot(a, b, dims=NN):
    return lax.dot_general(a, b, dims, preferred_element_type=jnp.float32)


def layer_kernel(
    size, width, x_ref, w_ref, wo_ref, k_ref, v_ref, len_ref, assign_ref, freq_ref, out_ref,
    xsort, xgot, xbuf, ranks_sum, rows_scale, wbuf, wall, obuf, oall, pbuf, prec, pown, kbuf, vbuf, qs, fresh, lens_sorted, scores,
    mall, ybuf, yrec, yown, zbuf, zrec,
    local_sem, s_send, s_recv, r_send, r_recv, x_send, x_recv, w_send, w_recv, wf_send, wf_recv, o_send, o_recv, of_send, of_recv,
    p_send, p_recv, m_send, m_recv, y_send, y_recv, z_send, z_recv,
):
    g = lax.axis_index("grp")
    t = lax.axis_index("tp")
    q, c = g // 2, g % 2
    rows = x_ref.shape[0]
    head_cols = (PER_KEY + 2) * HEAD_SIZE
    mixed_cols = PER_KEY * HEAD_SIZE
    piece = w_ref.shape[0]
    context = k_ref.shape[1]
    pairs = k_ref.shape[0] // 2

    sibling = (q * 2 + 1 - c, t)
    mirror = (t * 2 + c, q)

    def turn(value, k):
        return lax.rem(value + k, size)

    def rank_device(rank):
        return (g, rank)

    def chip_device(chip):
        return (chip * 2 + c, t)

    side = size // 2

    def across(value):
        return turn(value, side)

    def along(value, k):
        return value // side * side + lax.rem(lax.rem(value, side) + k, side)

    def remote(src, dst, send, recv, device):
        return pltpu.make_async_remote_copy(
            src_ref=src, dst_ref=dst, send_sem=send, recv_sem=recv, device_id=device, device_id_type=MESH
        )

    def await_into(ref, sem):
        pltpu.make_async_copy(ref, ref, sem).wait()

    barrier = pltpu.get_barrier_semaphore()

    def greet(device):
        pl.semaphore_signal(barrier, inc=1, device_id=device, device_id_type=MESH)

    for k in range(1, size):
        greet(rank_device(turn(t, k)))
        greet(chip_device(turn(q, k)))
        greet((t * 2 + c, turn(t, k)))
        greet((turn(q, k) * 2 + c, q))
    greet(sibling)

    @pl.when(q != t)
    def _():
        greet((t * 2 + c, t))
        greet((q * 2 + c, q))

    k_copy = pltpu.make_async_copy(k_ref, kbuf, local_sem.at[0])
    v_copy = pltpu.make_async_copy(v_ref, vbuf, local_sem.at[1])
    k_copy.start()
    v_copy.start()

    pl.semaphore_wait(barrier, jnp.where(q == t, 4 * size - 3, 4 * size - 1))

    def w_copy(k):
        cols = pl.ds(pl.multiple_of(turn(t, k) * head_cols, HEAD_SIZE), head_cols)
        return remote(w_ref.at[:, cols], wbuf.at[c, t], w_send.at[k], w_recv.at[t], rank_device(turn(t, k)))

    def o_copy(k):
        cols = pl.ds(pl.multiple_of(turn(t, k) * mixed_cols, HEAD_SIZE), mixed_cols)
        return remote(wo_ref.at[:, cols], obuf.at[c, t], o_send.at[k], o_recv.at[t], rank_device(turn(t, k)))

    own_cols = pl.ds(pl.multiple_of(t * head_cols, HEAD_SIZE), head_cols)
    own_w = pltpu.make_async_copy(w_ref.at[:, own_cols], wbuf.at[c, t], w_recv.at[t])
    own_mixed = pl.ds(pl.multiple_of(t * mixed_cols, HEAD_SIZE), mixed_cols)
    own_o = pltpu.make_async_copy(wo_ref.at[:, own_mixed], obuf.at[c, t], o_recv.at[t])

    own_w.start()
    own_o.start()
    for k in range(1, size):
        w_copy(k).start()

    assign_row = jnp.broadcast_to(assign_ref[...], (rows, rows))
    i_row = lax.broadcasted_iota(jnp.int32, (rows, rows), 0)
    i_col = lax.broadcasted_iota(jnp.int32, (rows, rows), 1)
    diagonal = i_row == i_col

    def column(row_values):
        return jnp.sum(jnp.where(diagonal, row_values, 0.0), axis=1, keepdims=True)

    assign_f = assign_row.astype(jnp.float32)
    same = assign_f == column(assign_f)
    earlier = jnp.sum(jnp.where(same, jnp.where(i_row < i_col, 1.0, 0.0), 0.0), axis=0, keepdims=True)
    place_row = assign_f * SAMPLES + earlier
    place_col = column(place_row)
    sort_mat = jnp.where(i_row.astype(jnp.float32) == place_row, 1.0, 0.0)
    back_mat = jnp.where(i_col.astype(jnp.float32) == place_col, 1.0, 0.0).astype(jnp.bfloat16)
    lens = jnp.sum(sort_mat * len_ref[...].astype(jnp.float32), axis=1, keepdims=True)
    lens_sorted[...] = jnp.broadcast_to(lens, (rows, HEAD_SIZE))
    sort_mat = sort_mat.astype(jnp.bfloat16)

    xsort[...] = dot(sort_mat, x_ref[...]).astype(jnp.bfloat16)

    def x_copy(k):
        return remote(xsort, xgot.at[q], x_send.at[k], x_recv.at[q], (t * 2 + c, turn(t, k)))

    own_x = pltpu.make_async_copy(xsort, xgot.at[q], x_recv.at[q])

    @pl.when(q == t)
    def _():
        own_x.start()

    @pl.when(q != t)
    def _():
        x_copy(0).start()

    for k in range(1, size):
        x_copy(k).start()

    lane_diagonal = lax.broadcasted_iota(jnp.int32, (rows, HEAD_SIZE), 0) == lax.broadcasted_iota(
        jnp.int32, (rows, HEAD_SIZE), 1
    )

    def s_copy(k):
        return remote(ranks_sum.at[t], ranks_sum.at[t], s_send.at[k], s_recv.at[t], rank_device(turn(t, k)))

    def r_copy(k):
        return remote(rows_scale.at[q], rows_scale.at[q], r_send.at[k], r_recv.at[q], chip_device(turn(q, k)))

    features = xsort[...].astype(jnp.float32)
    squares = jnp.sum(features * features, axis=-1, keepdims=True)
    ranks_sum[t] = jnp.broadcast_to(
        jnp.sum(jnp.where(lane_diagonal, squares, 0.0), axis=0, keepdims=True), (8, HEAD_SIZE)
    )
    for k in range(1, size):
        s_copy(k).start()

    angle = lens * freq_ref[...]
    lane = lax.broadcasted_iota(jnp.int32, (rows, HEAD_SIZE), 1)
    cosine = jnp.cos(angle)
    sine = jnp.where(lane < HEAD_SIZE // 2, -1.0, 1.0) * jnp.sin(angle)

    for k in range(1, size):
        await_into(ranks_sum.at[turn(t, k)], s_recv.at[turn(t, k)])
    total = ranks_sum[0]
    for s in range(1, size):
        total = total + ranks_sum[s]
    rows_scale[q] = lax.rsqrt(total * (1.0 / width) + EPS)
    for k in range(1, size):
        r_copy(k).start()

    def wf_copy(s):
        return remote(wbuf.at[c, s], wbuf.at[c, s], wf_send.at[s], wf_recv.at[s], sibling)

    def of_copy(s):
        return remote(obuf.at[c, s], obuf.at[c, s], of_send.at[s], of_recv.at[s], sibling)

    for s in range(size):
        await_into(wbuf.at[c, s], w_recv.at[s])
        wf_copy(s).start()
    for s in range(size):
        await_into(wbuf.at[1 - c, s], wf_recv.at[s])
    for core in range(2):
        for s in range(size):
            first = (core * size + s) * piece
            wall[first : first + piece, :] = wbuf[core, s]

    half_rows = rows // 2
    halves = [slice(half * half_rows, (half + 1) * half_rows) for half in range(2)]

    def p_copy(half, chip):
        return remote(
            pbuf.at[half, chip], prec.at[half, q], p_send.at[half, chip], p_recv.at[half, q], chip_device(chip)
        )

    for k in range(1, size):
        await_into(rows_scale.at[turn(q, k)], r_recv.at[turn(q, k)])
    for chip in range(size):
        await_into(xgot.at[chip], x_recv.at[chip])
        scale = jnp.sum(jnp.where(lane_diagonal, rows_scale[chip, :1], 0.0), axis=1, keepdims=True)
        xbuf[chip] = (xgot[chip].astype(jnp.float32) * scale).astype(jnp.bfloat16)

    def project(half):
        def step(k, carry):
            first = lax.rem(q // 2 + k, side) * 2
            block = xbuf[pl.ds(first, 2), halves[half], :].reshape(rows, -1)
            block = dot(block, wall[...])
            for part in range(2):
                chip = first + part

                @pl.when(chip == q)
                def _():
                    pown[half] = block[halves[part]]

                @pl.when(chip != q)
                def _():
                    pbuf[half, chip] = block[halves[part]].astype(pbuf.dtype)
                    p_copy(half, chip).start()

            return carry

        lax.fori_loop(1, side + 1, step, 0)

    project(0)
    project(1)

    def prepare(half):
        for k in range(1, size):
            await_into(prec.at[half, turn(q, k)], p_recv.at[half, turn(q, k)])
        for h in range(PER_KEY + 2):
            cols = slice(h * HEAD_SIZE, (h + 1) * HEAD_SIZE)
            head = pown[half, :, cols]
            for k in range(1, size):
                head = head + prec[half, turn(q, k), :, cols].astype(jnp.float32)
            if h <= PER_KEY:
                head = head * lax.rsqrt(jnp.mean(head * head, axis=-1, keepdims=True) + EPS)
                rolled = pltpu.roll(head, HEAD_SIZE // 2, 1)
                head = head * cosine[halves[half]] + rolled * sine[halves[half]]
            head = head.astype(jnp.bfloat16).astype(jnp.float32)
            if h < PER_KEY:
                qs[h, halves[half], :] = head
            else:
                fresh[h - PER_KEY, halves[half], :] = head

    scale2 = HEAD_SIZE ** (-0.5) * LOG2E
    queries = PER_KEY * SAMPLES
    slot_iota = lax.broadcasted_iota(jnp.int32, (queries, HEAD_SIZE), 1).astype(jnp.float32)

    def attend(p):
        mine = pl.ds(pl.multiple_of(p * SAMPLES, SAMPLES), SAMPLES)
        query = qs[:, mine, :]
        own = jnp.sum(query * fresh[0, mine, :][None], axis=-1, keepdims=True).reshape(queries, 1)
        fresh_value = jnp.broadcast_to(fresh[1, mine, :][None], query.shape).reshape(queries, HEAD_SIZE)
        seen = jnp.broadcast_to(lens_sorted[mine, :][None], query.shape).reshape(queries, HEAD_SIZE)
        query = query.reshape(queries, HEAD_SIZE).astype(jnp.bfloat16)
        top = jnp.full((queries, HEAD_SIZE), MASKED, jnp.float32)
        for chunk in range(context // CHUNK):
            part = dot(query, kbuf[p, chunk * CHUNK : (chunk + 1) * CHUNK, :], NT)
            for lane in range(CHUNK // HEAD_SIZE):
                first = chunk * CHUNK + lane * HEAD_SIZE
                tile = part[:, lane * HEAD_SIZE : (lane + 1) * HEAD_SIZE]
                tile = jnp.where(slot_iota < seen - first, tile, MASKED)
                scores[:, first : first + HEAD_SIZE] = tile
                top = jnp.maximum(top, tile)
        peak = jnp.maximum(jnp.max(top, axis=-1, keepdims=True), own)
        shift = peak * scale2
        own_weight = jnp.exp2(own * scale2 - shift)
        sums = jnp.zeros((queries, HEAD_SIZE), jnp.float32)
        for chunk in range(context // CHUNK):
            cols = slice(chunk * CHUNK, (chunk + 1) * CHUNK)
            weights = jnp.exp2(scores[:, cols] * scale2 - shift)
            scores[:, cols] = weights
            for lane in range(CHUNK // HEAD_SIZE):
                sums = sums + weights[:, lane * HEAD_SIZE : (lane + 1) * HEAD_SIZE]
        part = 1.0 / (jnp.sum(sums, axis=-1, keepdims=True) + own_weight)
        mixed = (own_weight * part).astype(jnp.bfloat16).astype(jnp.float32) * fresh_value
        for chunk in range(context // CHUNK):
            cols = slice(chunk * CHUNK, (chunk + 1) * CHUNK)
            mixed = mixed + dot((scores[:, cols] * part).astype(jnp.bfloat16), vbuf[p, cols, :])
        return mixed

    def m_copy(i, source, chip, sem):
        return remote(
            mall.at[source, i], mall.at[source, i], m_send.at[i, sem], m_recv.at[i, source], chip_device(chip)
        )

    def m_across(i):
        return m_copy(i, q, across(q), 0)

    def m_own(i, k):
        return m_copy(i, q, along(q, k), k)

    def m_passed(i, k):
        return m_copy(i, across(q), along(q, k), side + k)

    def pass_on(i):
        await_into(mall.at[across(q), i], m_recv.at[i, across(q)])
        for k in range(1, side):
            m_passed(i, k).start()

    def attend_pair(i, carry):
        low, high = attend(2 * i), attend(2 * i + 1)
        for h in range(PER_KEY):
            part = slice(h * SAMPLES, (h + 1) * SAMPLES)
            mall[q, i, :, h * HEAD_SIZE : (h + 1) * HEAD_SIZE] = jnp.concatenate(
                [low[part], high[part]], axis=0
            ).astype(jnp.bfloat16)
        m_across(i).start()
        for k in range(1, side):
            m_own(i, k).start()

        @pl.when(i > 0)
        def _():
            pass_on(i - 1)

        return carry

    prepare(0)
    for k in range(1, size):
        o_copy(k).start()
    k_copy.wait()
    v_copy.wait()
    lax.fori_loop(0, pairs // 2, attend_pair, 0)
    prepare(1)
    lax.fori_loop(pairs // 2, pairs - 1, attend_pair, 0)
    for s in range(size):
        await_into(obuf.at[c, s], o_recv.at[s])
        of_copy(s).start()
    attend_pair(pairs - 1, 0)
    pass_on(pairs - 1)
    for s in range(size):
        await_into(obuf.at[1 - c, s], of_recv.at[s])
    for core in range(2):
        for s in range(size):
            first = (core * size + s) * piece
            oall[first : first + piece, :] = obuf[core, s]

    def y_copy(half, rank):
        return remote(
            ybuf.at[half, rank], yrec.at[half, t], y_send.at[half, rank], y_recv.at[half, t], rank_device(rank)
        )

    half_pairs = pairs // 2

    def project_out(half):
        def step(k, carry):
            first = lax.rem(t // 2 + k, side) * 2
            for part in range(2):
                chip = first + part

                @pl.when((chip != q) & (chip != across(q)))
                def _():
                    for i in range(half * half_pairs, (half + 1) * half_pairs):
                        await_into(mall.at[chip, i], m_recv.at[i, chip])

            block = mall[pl.ds(first, 2), half * half_pairs : (half + 1) * half_pairs]
            block = dot(block.reshape(rows, mixed_cols), oall[...], NT)
            for part in range(2):
                rank = first + part

                @pl.when(rank == t)
                def _():
                    yown[half] = block[halves[part]]

                @pl.when(rank != t)
                def _():
                    ybuf[half, rank] = block[halves[part]].astype(ybuf.dtype)
                    y_copy(half, rank).start()

            return carry

        lax.fori_loop(1, side + 1, step, 0)

    def z_copy(half):
        return remote(zbuf.at[half], zrec.at[half], z_send.at[half], z_recv.at[half], mirror)

    project_out(0)
    project_out(1)
    for half in range(2):
        result = yown[half]
        for k in range(1, size):
            await_into(yrec.at[half, turn(t, k)], y_recv.at[half, turn(t, k)])
        for k in range(1, size):
            result = result + yrec[half, turn(t, k)].astype(jnp.float32)
        zbuf[half] = result.astype(jnp.bfloat16)

        @pl.when(q != t)
        def _():
            z_copy(half).start()

    @pl.when(q != t)
    def _():
        for half in range(2):
            z_copy(half).wait()

    @pl.when(q == t)
    def _():
        zrec[...] = zbuf[...]

    out_ref[...] = dot(back_mat, zrec[...].reshape(rows, -1)).astype(jnp.bfloat16)

    @pl.when(q != t)
    def _():
        x_copy(0).wait_send()

    for k in range(1, size):
        x_copy(k).wait_send()
        s_copy(k).wait_send()
        r_copy(k).wait_send()
        w_copy(k).wait_send()
        o_copy(k).wait_send()
        for half in range(2):
            p_copy(half, turn(q, k)).wait_send()
            y_copy(half, turn(t, k)).wait_send()
    for i in range(pairs):
        m_across(i).wait_send()
        for k in range(1, side):
            m_own(i, k).wait_send()
            m_passed(i, k).wait_send()
    for s in range(size):
        wf_copy(s).wait_send()
        of_copy(s).wait_send()


def local(size, hidden, query_key_value_weight, w_out, k_cache, value_cache, lengths, assign):
    rows, features = hidden.shape
    width = features * size
    piece = query_key_value_weight.shape[0]
    prompts, context = k_cache.shape[0], k_cache.shape[1]
    half = np.arange(HEAD_SIZE // 2, dtype=np.float32)
    freq = np.float32(ROPE_BASE) ** (-half * np.float32(2.0) / np.float32(HEAD_SIZE))
    freq = np.concatenate([freq, freq]).astype(np.float32)[None, :]
    head_cols = (PER_KEY + 2) * HEAD_SIZE
    mixed_cols = PER_KEY * HEAD_SIZE
    bf16, f32 = jnp.bfloat16, jnp.float32
    dma = pltpu.SemaphoreType.DMA
    pairs = prompts // 2
    vmem = pl.BlockSpec(memory_space=pltpu.VMEM)
    anywhere = pl.BlockSpec(memory_space=pl.ANY)
    return pl.pallas_call(
        functools.partial(layer_kernel, size, width),
        out_shape=jax.ShapeDtypeStruct((rows, features), bf16),
        in_specs=[vmem, anywhere, anywhere, anywhere, anywhere, vmem, vmem, vmem],
        out_specs=vmem,
        scratch_shapes=[
            pltpu.VMEM((rows, features), bf16),
            pltpu.VMEM((size, rows, features), bf16),
            pltpu.VMEM((size, rows, features), bf16),
            pltpu.VMEM((size, 8, HEAD_SIZE), f32),
            pltpu.VMEM((size, 8, HEAD_SIZE), f32),
            pltpu.VMEM((2, size, piece, head_cols), bf16),
            pltpu.VMEM((features, head_cols), bf16),
            pltpu.VMEM((2, size, piece, mixed_cols), bf16),
            pltpu.VMEM((features, mixed_cols), bf16),
            pltpu.VMEM((2, size, rows // 2, head_cols), P_TYPE),
            pltpu.VMEM((2, size, rows // 2, head_cols), P_TYPE),
            pltpu.VMEM((2, rows // 2, head_cols), f32),
            pltpu.VMEM((prompts, context, HEAD_SIZE), bf16),
            pltpu.VMEM((prompts, context, HEAD_SIZE), bf16),
            pltpu.VMEM((PER_KEY, rows, HEAD_SIZE), f32),
            pltpu.VMEM((2, rows, HEAD_SIZE), f32),
            pltpu.VMEM((rows, HEAD_SIZE), f32),
            pltpu.VMEM((PER_KEY * SAMPLES, context), f32),
            pltpu.VMEM((size, pairs, 2 * SAMPLES, mixed_cols), bf16),
            pltpu.VMEM((2, size, rows // 2, features), Y_TYPE),
            pltpu.VMEM((2, size, rows // 2, features), Y_TYPE),
            pltpu.VMEM((2, rows // 2, features), f32),
            pltpu.VMEM((2, rows // 2, features), bf16),
            pltpu.VMEM((2, rows // 2, features), bf16),
            dma((2,)),
            dma((size,)), dma((size,)), dma((size,)), dma((size,)),
            dma((size,)), dma((size,)),
            dma((size,)), dma((size,)), dma((size,)), dma((size,)),
            dma((size,)), dma((size,)), dma((size,)), dma((size,)),
            dma((2, size)), dma((2, size)),
            dma((pairs, size)), dma((pairs, size)),
            dma((2, size)), dma((2, size)),
            dma((2,)), dma((2,)),
        ],
        compiler_params=pltpu.CompilerParams(
            collective_id=0, has_side_effects=True, vmem_limit_bytes=56 * 1024 * 1024
        ),
        name="layer",
    )(
        hidden,
        query_key_value_weight,
        w_out.T,
        k_cache.reshape(prompts, context, HEAD_SIZE),
        value_cache.reshape(prompts, context, HEAD_SIZE),
        lengths.reshape(1, rows),
        assign.reshape(1, rows),
        jnp.asarray(freq),
    )


def solution(mesh):
    return jax.shard_map(
        functools.partial(local, mesh.shape["tp"]),
        mesh=mesh,
        in_specs=(
            P("grp", "tp"),
            P(("grp", "tp"), None),
            P(None, ("grp", "tp")),
            P("grp", None, "tp", None),
            P("grp", None, "tp", None),
            P("grp"),
            P("grp"),
        ),
        out_specs=P("grp", "tp"),
        check_vma=False,
    )
```

time: 95.7 us -> 85 us (0.89)
  the two profiles are of different devices: /device:TPU:6 before, /device:TPU:20 now
where the time goes in v3:
time: 85 us; the launch traced here: 84.1 us
  Pallas kernels  82.6 us (97%)
  local copies, waits for them, and re-layouts  1.53 us (2%)
    pallas_call x1, Pallas kernels, local(): pl.pallas_call(functools.partial(layer_kernel, size, width), out_shape=ja...  82.6 us

profile of v3, /device:TPU:20, one launch (start us, length us, event | category | flops | bytes accessed | tf_op | source)
XLA Modules:
  0.0 84.1 jit_solution(7318036851233260027)
XLA Ops:
  0.0 82.6 %layer.1 = bf16[64,640]{1,0:T(8,128)(2,1)} custom-call(bf16[64,640]{1,0:T(8,128)(2,1)} %x_ref.1, bf16[40,10240]{1,0:T(8,128)(2,1)} %w_ref.1, bf16[40,8192]{1,0:T(8,128)(2,1)} %bitcast.7, bf16[8,4096,128]{2,1,0:T(8,128)(2,1)} %bitcast.5, bf16[8,4096,128]{2,1,0:T(8,128)(2,1)} %bitcast.6, s32[1,64]{1,0:T(1,128)} %bitcast.8, s32[1,64]{1,0:T(1,128)} %bitcast.9, ...), custom_call_target="tpu_custom_call" | custom-call | tf_op jit(solution)/shard_map/layer/pallas_call | solution.py:455
  82.6 1.5 %copy.10 = bf16[64,640]{1,0:T(8,128)(2,1)} copy(bf16[64,640]{1,0:T(8,128)(2,1)} %layer.1) | data formatting | bytes 163840

commit v4 on v3

--- a/solution.py
+++ b/solution.py
@@ -46,7 +46,12 @@
     pairs = k_ref.shape[0] // 2
 
     sibling = (q * 2 + 1 - c, t)
-    mirror = (t * 2 + c, q)
+
+    def summing_rank(chip):
+        return chip % (size // 2) * 2 + chip // (size // 2)
+
+    summed_chip = t % 2 * (size // 2) + t // 2
+    alone = (summed_chip == q) & (q == t)
 
     def turn(value, k):
         return lax.rem(value + k, size)
@@ -94,26 +99,6 @@
     v_copy = pltpu.make_async_copy(v_ref, vbuf, local_sem.at[1])
     k_copy.start()
     v_copy.start()
-
-    pl.semaphore_wait(barrier, jnp.where(q == t, 4 * size - 3, 4 * size - 1))
-
-    def w_copy(k):
-        cols = pl.ds(pl.multiple_of(turn(t, k) * head_cols, HEAD_SIZE), head_cols)
-        return remote(w_ref.at[:, cols], wbuf.at[c, t], w_send.at[k], w_recv.at[t], rank_device(turn(t, k)))
-
-    def o_copy(k):
-        cols = pl.ds(pl.multiple_of(turn(t, k) * mixed_cols, HEAD_SIZE), mixed_cols)
-        return remote(wo_ref.at[:, cols], obuf.at[c, t], o_send.at[k], o_recv.at[t], rank_device(turn(t, k)))
-
-    own_cols = pl.ds(pl.multiple_of(t * head_cols, HEAD_SIZE), head_cols)
-    own_w = pltpu.make_async_copy(w_ref.at[:, own_cols], wbuf.at[c, t], w_recv.at[t])
-    own_mixed = pl.ds(pl.multiple_of(t * mixed_cols, HEAD_SIZE), mixed_cols)
-    own_o = pltpu.make_async_copy(wo_ref.at[:, own_mixed], obuf.at[c, t], o_recv.at[t])
-
-    own_w.start()
-    own_o.start()
-    for k in range(1, size):
-        w_copy(k).start()
 
     assign_row = jnp.broadcast_to(assign_ref[...], (rows, rows))
     i_row = lax.broadcasted_iota(jnp.int32, (rows, rows), 0)
@@ -136,39 +121,69 @@
 
     xsort[...] = dot(sort_mat, x_ref[...]).astype(jnp.bfloat16)
 
-    def x_copy(k):
-        return remote(xsort, xgot.at[q], x_send.at[k], x_recv.at[q], (t * 2 + c, turn(t, k)))
-
-    own_x = pltpu.make_async_copy(xsort, xgot.at[q], x_recv.at[q])
-
-    @pl.when(q == t)
-    def _():
-        own_x.start()
-
-    @pl.when(q != t)
-    def _():
-        x_copy(0).start()
-
-    for k in range(1, size):
-        x_copy(k).start()
-
     lane_diagonal = lax.broadcasted_iota(jnp.int32, (rows, HEAD_SIZE), 0) == lax.broadcasted_iota(
         jnp.int32, (rows, HEAD_SIZE), 1
     )
-
-    def s_copy(k):
-        return remote(ranks_sum.at[t], ranks_sum.at[t], s_send.at[k], s_recv.at[t], rank_device(turn(t, k)))
-
-    def r_copy(k):
-        return remote(rows_scale.at[q], rows_scale.at[q], r_send.at[k], r_recv.at[q], chip_device(turn(q, k)))
 
     features = xsort[...].astype(jnp.float32)
     squares = jnp.sum(features * features, axis=-1, keepdims=True)
     ranks_sum[t] = jnp.broadcast_to(
         jnp.sum(jnp.where(lane_diagonal, squares, 0.0), axis=0, keepdims=True), (8, HEAD_SIZE)
     )
+
+    pl.semaphore_wait(barrier, jnp.where(q == t, 4 * size - 3, 4 * size - 1))
+
+    part_cols = head_cols // 2
+
+    def w_cols(part, rank):
+        return pl.ds(pl.multiple_of(rank * head_cols + part * part_cols, HEAD_SIZE), part_cols)
+
+    def w_copy(part, k):
+        rank = turn(t, k)
+        return remote(
+            w_ref.at[:, w_cols(part, rank)], wbuf.at[part, c, t], w_send.at[part, k], w_recv.at[part, t], rank_device(rank)
+        )
+
+    def o_copy(k):
+        cols = pl.ds(pl.multiple_of(turn(t, k) * mixed_cols, HEAD_SIZE), mixed_cols)
+        return remote(wo_ref.at[:, cols], obuf.at[c, t], o_send.at[k], o_recv.at[t], rank_device(turn(t, k)))
+
+    def own_w(part):
+        return pltpu.make_async_copy(w_ref.at[:, w_cols(part, t)], wbuf.at[part, c, t], w_recv.at[part, t])
+
+    own_mixed = pl.ds(pl.multiple_of(t * mixed_cols, HEAD_SIZE), mixed_cols)
+    own_o = pltpu.make_async_copy(wo_ref.at[:, own_mixed], obuf.at[c, t], o_recv.at[t])
+
+    def x_copy(k):
+        return remote(xsort, xgot.at[q], x_send.at[k], x_recv.at[q], (t * 2 + c, turn(t, k)))
+
+    own_x = pltpu.make_async_copy(xsort, xgot.at[q], x_recv.at[q])
+
+    @pl.when(q == t)
+    def _():
+        own_x.start()
+
+    @pl.when(q != t)
+    def _():
+        x_copy(0).start()
+
+    for k in range(1, size):
+        x_copy(k).start()
+
+    def s_copy(k):
+        return remote(ranks_sum.at[t], ranks_sum.at[t], s_send.at[k], s_recv.at[t], rank_device(turn(t, k)))
+
+    def r_copy(k):
+        return remote(rows_scale.at[q], rows_scale.at[q], r_send.at[k], r_recv.at[q], chip_device(turn(q, k)))
+
     for k in range(1, size):
         s_copy(k).start()
+
+    for part in range(2):
+        own_w(part).start()
+        for k in range(1, size):
+            w_copy(part, k).start()
+    own_o.start()
 
     angle = lens * freq_ref[...]
     lane = lax.broadcasted_iota(jnp.int32, (rows, HEAD_SIZE), 1)
@@ -184,28 +199,37 @@
     for k in range(1, size):
         r_copy(k).start()
 
-    def wf_copy(s):
-        return remote(wbuf.at[c, s], wbuf.at[c, s], wf_send.at[s], wf_recv.at[s], sibling)
+    def wf_copy(part, s):
+        piece_at = wbuf.at[part, c, s]
+        return remote(piece_at, piece_at, wf_send.at[part, s], wf_recv.at[part, s], sibling)
 
     def of_copy(s):
         return remote(obuf.at[c, s], obuf.at[c, s], of_send.at[s], of_recv.at[s], sibling)
 
-    for s in range(size):
-        await_into(wbuf.at[c, s], w_recv.at[s])
-        wf_copy(s).start()
-    for s in range(size):
-        await_into(wbuf.at[1 - c, s], wf_recv.at[s])
-    for core in range(2):
+    def gather_weights(part):
+        for k in range(size):
+            s = turn(t, size - k)
+            await_into(wbuf.at[part, c, s], w_recv.at[part, s])
+            wf_copy(part, s).start()
         for s in range(size):
-            first = (core * size + s) * piece
-            wall[first : first + piece, :] = wbuf[core, s]
+            await_into(wbuf.at[part, 1 - c, s], wf_recv.at[part, s])
+        for core in range(2):
+            for s in range(size):
+                first = (core * size + s) * piece
+                wall[part, first : first + piece, :] = wbuf[part, core, s]
+
+    gather_weights(0)
 
     half_rows = rows // 2
     halves = [slice(half * half_rows, (half + 1) * half_rows) for half in range(2)]
 
-    def p_copy(half, chip):
+    def p_copy(part, half, chip):
         return remote(
-            pbuf.at[half, chip], prec.at[half, q], p_send.at[half, chip], p_recv.at[half, q], chip_device(chip)
+            pbuf.at[part, half, chip],
+            prec.at[part, half, q],
+            p_send.at[part, half, chip],
+            p_recv.at[part, half, q],
+            chip_device(chip),
         )
 
     for k in range(1, size):
@@ -215,38 +239,36 @@
         scale = jnp.sum(jnp.where(lane_diagonal, rows_scale[chip, :1], 0.0), axis=1, keepdims=True)
         xbuf[chip] = (xgot[chip].astype(jnp.float32) * scale).astype(jnp.bfloat16)
 
-    def project(half):
-        def step(k, carry):
-            first = lax.rem(q // 2 + k, side) * 2
-            block = xbuf[pl.ds(first, 2), halves[half], :].reshape(rows, -1)
-            block = dot(block, wall[...])
-            for part in range(2):
-                chip = first + part
-
-                @pl.when(chip == q)
-                def _():
-                    pown[half] = block[halves[part]]
-
-                @pl.when(chip != q)
-                def _():
-                    pbuf[half, chip] = block[halves[part]].astype(pbuf.dtype)
-                    p_copy(half, chip).start()
-
-            return carry
-
-        lax.fori_loop(1, side + 1, step, 0)
-
-    project(0)
-    project(1)
+    def project(part, half):
+        block = dot(xbuf[:, halves[half], :].reshape(size * half_rows, -1), wall[part])
+        for chip in range(size):
+            result = block[chip * half_rows : (chip + 1) * half_rows]
+
+            @pl.when(chip == q)
+            def _():
+                pown[part, half] = result
+
+            @pl.when(chip != q)
+            def _():
+                pbuf[part, half, chip] = result.astype(pbuf.dtype)
+                p_copy(part, half, chip).start()
+
+    project(0, 0)
+    gather_weights(1)
+    project(1, 0)
+    project(0, 1)
+    project(1, 1)
 
     def prepare(half):
         for k in range(1, size):
-            await_into(prec.at[half, turn(q, k)], p_recv.at[half, turn(q, k)])
+            for part in range(2):
+                await_into(prec.at[part, half, turn(q, k)], p_recv.at[part, half, turn(q, k)])
         for h in range(PER_KEY + 2):
-            cols = slice(h * HEAD_SIZE, (h + 1) * HEAD_SIZE)
-            head = pown[half, :, cols]
+            part, place = divmod(h, (PER_KEY + 2) // 2)
+            cols = slice(place * HEAD_SIZE, (place + 1) * HEAD_SIZE)
+            head = pown[part, half, :, cols]
             for k in range(1, size):
-                head = head + prec[half, turn(q, k), :, cols].astype(jnp.float32)
+                head = head + prec[part, half, turn(q, k), :, cols].astype(jnp.float32)
             if h <= PER_KEY:
                 head = head * lax.rsqrt(jnp.mean(head * head, axis=-1, keepdims=True) + EPS)
                 rolled = pltpu.roll(head, HEAD_SIZE // 2, 1)
@@ -313,35 +335,33 @@
         for k in range(1, side):
             m_passed(i, k).start()
 
-    def attend_pair(i, carry):
+    def attend_pair(i):
         low, high = attend(2 * i), attend(2 * i + 1)
         for h in range(PER_KEY):
             part = slice(h * SAMPLES, (h + 1) * SAMPLES)
             mall[q, i, :, h * HEAD_SIZE : (h + 1) * HEAD_SIZE] = jnp.concatenate(
                 [low[part], high[part]], axis=0
             ).astype(jnp.bfloat16)
+
+    prepare(0)
+    k_copy.wait()
+    v_copy.wait()
+    for i in range(pairs):
+        if i == 1:
+            for k in range(1, size):
+                o_copy(k).start()
+        if i == pairs // 2:
+            prepare(1)
+        if i == pairs - 1:
+            for s in range(size):
+                await_into(obuf.at[c, s], o_recv.at[s])
+                of_copy(s).start()
+        attend_pair(i)
         m_across(i).start()
         for k in range(1, side):
             m_own(i, k).start()
-
-        @pl.when(i > 0)
-        def _():
+        if i > 0:
             pass_on(i - 1)
-
-        return carry
-
-    prepare(0)
-    for k in range(1, size):
-        o_copy(k).start()
-    k_copy.wait()
-    v_copy.wait()
-    lax.fori_loop(0, pairs // 2, attend_pair, 0)
-    prepare(1)
-    lax.fori_loop(pairs // 2, pairs - 1, attend_pair, 0)
-    for s in range(size):
-        await_into(obuf.at[c, s], o_recv.at[s])
-        of_copy(s).start()
-    attend_pair(pairs - 1, 0)
     pass_on(pairs - 1)
     for s in range(size):
         await_into(obuf.at[1 - c, s], of_recv.at[s])
@@ -358,36 +378,30 @@
     half_pairs = pairs // 2
 
     def project_out(half):
-        def step(k, carry):
-            first = lax.rem(t // 2 + k, side) * 2
-            for part in range(2):
-                chip = first + part
+        for chip in range(size):
+            for i in range(half * half_pairs, (half + 1) * half_pairs):
 
                 @pl.when((chip != q) & (chip != across(q)))
                 def _():
-                    for i in range(half * half_pairs, (half + 1) * half_pairs):
-                        await_into(mall.at[chip, i], m_recv.at[i, chip])
-
-            block = mall[pl.ds(first, 2), half * half_pairs : (half + 1) * half_pairs]
-            block = dot(block.reshape(rows, mixed_cols), oall[...], NT)
-            for part in range(2):
-                rank = first + part
-
-                @pl.when(rank == t)
-                def _():
-                    yown[half] = block[halves[part]]
-
-                @pl.when(rank != t)
-                def _():
-                    ybuf[half, rank] = block[halves[part]].astype(ybuf.dtype)
-                    y_copy(half, rank).start()
-
-            return carry
-
-        lax.fori_loop(1, side + 1, step, 0)
+                    await_into(mall.at[chip, i], m_recv.at[i, chip])
+
+        block = mall[:, half * half_pairs : (half + 1) * half_pairs].reshape(size * half_rows, mixed_cols)
+        block = dot(block, oall[...], NT)
+        for chip in range(size):
+            rank = summing_rank(chip)
+            result = block[chip * half_rows : (chip + 1) * half_rows]
+
+            @pl.when(rank == t)
+            def _():
+                yown[half] = result
+
+            @pl.when(rank != t)
+            def _():
+                ybuf[half, rank] = result.astype(ybuf.dtype)
+                y_copy(half, rank).start()
 
     def z_copy(half):
-        return remote(zbuf.at[half], zrec.at[half], z_send.at[half], z_recv.at[half], mirror)
+        return remote(zbuf.at[half], zrec.at[half], z_send.at[half], z_recv.at[half], (summed_chip * 2 + c, q))
 
     project_out(0)
     project_out(1)
@@ -399,16 +413,16 @@
             result = result + yrec[half, turn(t, k)].astype(jnp.float32)
         zbuf[half] = result.astype(jnp.bfloat16)
 
-        @pl.when(q != t)
+        @pl.when(jnp.logical_not(alone))
         def _():
             z_copy(half).start()
 
-    @pl.when(q != t)
+    @pl.when(jnp.logical_not(alone))
     def _():
         for half in range(2):
             z_copy(half).wait()
 
-    @pl.when(q == t)
+    @pl.when(alone)
     def _():
         zrec[...] = zbuf[...]
 
@@ -422,10 +436,12 @@
         x_copy(k).wait_send()
         s_copy(k).wait_send()
         r_copy(k).wait_send()
-        w_copy(k).wait_send()
+        for part in range(2):
+            w_copy(part, k).wait_send()
         o_copy(k).wait_send()
         for half in range(2):
-            p_copy(half, turn(q, k)).wait_send()
+            for part in range(2):
+                p_copy(part, half, turn(q, k)).wait_send()
             y_copy(half, turn(t, k)).wait_send()
     for i in range(pairs):
         m_across(i).wait_send()
@@ -433,7 +449,8 @@
             m_own(i, k).wait_send()
             m_passed(i, k).wait_send()
     for s in range(size):
-        wf_copy(s).wait_send()
+        for part in range(2):
+            wf_copy(part, s).wait_send()
         of_copy(s).wait_send()
 
 
@@ -463,13 +480,13 @@
             pltpu.VMEM((size, rows, features), bf16),
             pltpu.VMEM((size, 8, HEAD_SIZE), f32),
             pltpu.VMEM((size, 8, HEAD_SIZE), f32),
-            pltpu.VMEM((2, size, piece, head_cols), bf16),
-            pltpu.VMEM((features, head_cols), bf16),
+            pltpu.VMEM((2, 2, size, piece, head_cols // 2), bf16),
+            pltpu.VMEM((2, features, head_cols // 2), bf16),
             pltpu.VMEM((2, size, piece, mixed_cols), bf16),
             pltpu.VMEM((features, mixed_cols), bf16),
-            pltpu.VMEM((2, size, rows // 2, head_cols), P_TYPE),
-            pltpu.VMEM((2, size, rows // 2, head_cols), P_TYPE),
-            pltpu.VMEM((2, rows // 2, head_cols), f32),
+            pltpu.VMEM((2, 2, size, rows // 2, head_cols // 2), P_TYPE),
+            pltpu.VMEM((2, 2, size, rows // 2, head_cols // 2), P_TYPE),
+            pltpu.VMEM((2, 2, rows // 2, head_cols // 2), f32),
             pltpu.VMEM((prompts, context, HEAD_SIZE), bf16),
             pltpu.VMEM((prompts, context, HEAD_SIZE), bf16),
             pltpu.VMEM((PER_KEY, rows, HEAD_SIZE), f32),
@@ -485,9 +502,9 @@
             dma((2,)),
             dma((size,)), dma((size,)), dma((size,)), dma((size,)),
             dma((size,)), dma((size,)),
+            dma((2, size)), dma((2, size)), dma((2, size)), dma((2, size)),
             dma((size,)), dma((size,)), dma((size,)), dma((size,)),
-            dma((size,)), dma((size,)), dma((size,)), dma((size,)),
-            dma((2, size)), dma((2, size)),
+            dma((2, 2, size)), dma((2, 2, size)),
             dma((pairs, size)), dma((pairs, size)),
             dma((2, size)), dma((2, size)),
             dma((2,)), dma((2,)),

time: 85 us -> 80.3 us (0.945)
  Pallas kernels: 82.6 us -> 78.6 us
    pallas_call x1, Pallas kernels: 82.6 us -> 78.6 us  [local(): pl.pallas_call(functools.partial(layer_kernel, size, width), out_shape=ja...]
where the time goes in v4:
time: 80.3 us; the launch traced here: 80.1 us
  Pallas kernels  78.6 us (98%)
  local copies, waits for them, and re-layouts  1.53 us (2%)
    pallas_call x1, Pallas kernels, local(): pl.pallas_call(functools.partial(layer_kernel, size, width), out_shape=ja...  78.6 us

profile of v4, /device:TPU:20, one launch (start us, length us, event | category | flops | bytes accessed | tf_op | source)
XLA Modules:
  0.0 80.1 jit_solution(13088638531803526593)
XLA Ops:
  0.0 78.6 %layer.1 = bf16[64,640]{1,0:T(8,128)(2,1)} custom-call(bf16[64,640]{1,0:T(8,128)(2,1)} %x_ref.1, bf16[40,10240]{1,0:T(8,128)(2,1)} %w_ref.1, bf16[40,8192]{1,0:T(8,128)(2,1)} %bitcast.7, bf16[8,4096,128]{2,1,0:T(8,128)(2,1)} %bitcast.5, bf16[8,4096,128]{2,1,0:T(8,128)(2,1)} %bitcast.6, s32[1,64]{1,0:T(1,128)} %bitcast.8, s32[1,64]{1,0:T(1,128)} %bitcast.9, ...), custom_call_target="tpu_custom_call" | custom-call | tf_op jit(solution)/shard_map/layer/pallas_call | solution.py:472
  78.6 1.5 %copy.10 = bf16[64,640]{1,0:T(8,128)(2,1)} copy(bf16[64,640]{1,0:T(8,128)(2,1)} %layer.1) | data formatting | bytes 163840

commit v5 on v4

--- a/solution.py
+++ b/solution.py
@@ -29,7 +29,8 @@
 
 
 def layer_kernel(
-    size, width, x_ref, w_ref, wo_ref, k_ref, v_ref, len_ref, assign_ref, freq_ref, out_ref,
+    size, width, x_hbm, w_ref, wo_ref, k_ref, v_ref, len_hbm, assign_hbm, freq_hbm, out_ref,
+    x_ref, len_ref, assign_ref, freq_ref,
     xsort, xgot, xbuf, ranks_sum, rows_scale, wbuf, wall, obuf, oall, pbuf, prec, pown, kbuf, vbuf, qs, fresh, lens_sorted, scores,
     mall, ybuf, yrec, yown, zbuf, zrec,
     local_sem, s_send, s_recv, r_send, r_recv, x_send, x_recv, w_send, w_recv, wf_send, wf_recv, o_send, o_recv, of_send, of_recv,
@@ -95,10 +96,21 @@
         greet((t * 2 + c, t))
         greet((q * 2 + c, q))
 
+    small = [
+        pltpu.make_async_copy(source, goal, local_sem.at[2 + i])
+        for i, (source, goal) in enumerate(
+            [(assign_hbm, assign_ref), (x_hbm, x_ref), (len_hbm, len_ref), (freq_hbm, freq_ref)]
+        )
+    ]
+    for copy in small:
+        copy.start()
     k_copy = pltpu.make_async_copy(k_ref, kbuf, local_sem.at[0])
     v_copy = pltpu.make_async_copy(v_ref, vbuf, local_sem.at[1])
     k_copy.start()
     v_copy.start()
+
+    for copy in small:
+        copy.wait()
 
     assign_row = jnp.broadcast_to(assign_ref[...], (rows, rows))
     i_row = lax.broadcasted_iota(jnp.int32, (rows, rows), 0)
@@ -206,11 +218,21 @@
     def of_copy(s):
         return remote(obuf.at[c, s], obuf.at[c, s], of_send.at[s], of_recv.at[s], sibling)
 
+    def norm_rows():
+        for k in range(1, size):
+            await_into(rows_scale.at[turn(q, k)], r_recv.at[turn(q, k)])
+        for chip in range(size):
+            await_into(xgot.at[chip], x_recv.at[chip])
+            scale = jnp.sum(jnp.where(lane_diagonal, rows_scale[chip, :1], 0.0), axis=1, keepdims=True)
+            xbuf[chip] = (xgot[chip].astype(jnp.float32) * scale).astype(jnp.bfloat16)
+
     def gather_weights(part):
         for k in range(size):
             s = turn(t, size - k)
             await_into(wbuf.at[part, c, s], w_recv.at[part, s])
             wf_copy(part, s).start()
+        if part == 0:
+            norm_rows()
         for s in range(size):
             await_into(wbuf.at[part, 1 - c, s], wf_recv.at[part, s])
         for core in range(2):
@@ -231,13 +253,6 @@
             p_recv.at[part, half, q],
             chip_device(chip),
         )
-
-    for k in range(1, size):
-        await_into(rows_scale.at[turn(q, k)], r_recv.at[turn(q, k)])
-    for chip in range(size):
-        await_into(xgot.at[chip], x_recv.at[chip])
-        scale = jnp.sum(jnp.where(lane_diagonal, rows_scale[chip, :1], 0.0), axis=1, keepdims=True)
-        xbuf[chip] = (xgot[chip].astype(jnp.float32) * scale).astype(jnp.bfloat16)
 
     def project(part, half):
         block = dot(xbuf[:, halves[half], :].reshape(size * half_rows, -1), wall[part])
@@ -472,9 +487,13 @@
     return pl.pallas_call(
         functools.partial(layer_kernel, size, width),
         out_shape=jax.ShapeDtypeStruct((rows, features), bf16),
-        in_specs=[vmem, anywhere, anywhere, anywhere, anywhere, vmem, vmem, vmem],
+        in_specs=[anywhere] * 8,
         out_specs=vmem,
         scratch_shapes=[
+            pltpu.VMEM((rows, features), bf16),
+            pltpu.VMEM((1, rows), jnp.int32),
+            pltpu.VMEM((1, rows), jnp.int32),
+            pltpu.VMEM((1, HEAD_SIZE), f32),
             pltpu.VMEM((rows, features), bf16),
             pltpu.VMEM((size, rows, features), bf16),
             pltpu.VMEM((size, rows, features), bf16),
@@ -499,7 +518,7 @@
             pltpu.VMEM((2, rows // 2, features), f32),
             pltpu.VMEM((2, rows // 2, features), bf16),
             pltpu.VMEM((2, rows // 2, features), bf16),
-            dma((2,)),
+            dma((6,)),
             dma((size,)), dma((size,)), dma((size,)), dma((size,)),
             dma((size,)), dma((size,)),
             dma((2, size)), dma((2, size)), dma((2, size)), dma((2, size)),

time: 80.3 us -> 79.3 us (0.988)
  Pallas kernels: 78.6 us -> 77.6 us
    pallas_call x1, Pallas kernels: 78.6 us -> 77.6 us  [local(): pl.pallas_call(functools.partial(layer_kernel, size, width), out_shape=ja...]
where the time goes in v5:
time: 79.3 us; the launch traced here: 79.1 us
  Pallas kernels  77.6 us (98%)
  local copies, waits for them, and re-layouts  1.53 us (2%)
    pallas_call x1, Pallas kernels, local(): pl.pallas_call(functools.partial(layer_kernel, size, width), out_shape=ja...  77.6 us

profile of v5, /device:TPU:20, one launch (start us, length us, event | category | flops | bytes accessed | tf_op | source)
XLA Modules:
  0.0 79.1 jit_solution(13520014531060216733)
XLA Ops:
  0.0 77.6 %layer.1 = bf16[64,640]{1,0:T(8,128)(2,1)} custom-call(bf16[64,640]{1,0:T(8,128)(2,1)} %x_hbm.1, bf16[40,10240]{1,0:T(8,128)(2,1)} %w_ref.1, bf16[40,8192]{1,0:T(8,128)(2,1)} %bitcast.7, bf16[8,4096,128]{2,1,0:T(8,128)(2,1)} %bitcast.5, bf16[8,4096,128]{2,1,0:T(8,128)(2,1)} %bitcast.6, s32[1,64]{1,0:T(1,128)} %bitcast.8, s32[1,64]{1,0:T(1,128)} %bitcast.9, ...), custom_call_target="tpu_custom_call" | custom-call | tf_op jit(solution)/shard_map/layer/pallas_call | solution.py:487
  77.6 1.5 %copy.10 = bf16[64,640]{1,0:T(8,128)(2,1)} copy(bf16[64,640]{1,0:T(8,128)(2,1)} %layer.1) | data formatting | bytes 163840

commit v6 on v5

--- a/solution.py
+++ b/solution.py
@@ -124,9 +124,7 @@
     same = assign_f == column(assign_f)
     earlier = jnp.sum(jnp.where(same, jnp.where(i_row < i_col, 1.0, 0.0), 0.0), axis=0, keepdims=True)
     place_row = assign_f * SAMPLES + earlier
-    place_col = column(place_row)
     sort_mat = jnp.where(i_row.astype(jnp.float32) == place_row, 1.0, 0.0)
-    back_mat = jnp.where(i_col.astype(jnp.float32) == place_col, 1.0, 0.0).astype(jnp.bfloat16)
     lens = jnp.sum(sort_mat * len_ref[...].astype(jnp.float32), axis=1, keepdims=True)
     lens_sorted[...] = jnp.broadcast_to(lens, (rows, HEAD_SIZE))
     sort_mat = sort_mat.astype(jnp.bfloat16)
@@ -441,7 +439,8 @@
     def _():
         zrec[...] = zbuf[...]
 
-    out_ref[...] = dot(back_mat, zrec[...].reshape(rows, -1)).astype(jnp.bfloat16)
+    for half in range(2):
+        out_ref[halves[half], :] = zrec[half]
 
     @pl.when(q != t)
     def _():
@@ -469,6 +468,18 @@
         of_copy(s).wait_send()
 
 
+def restore_kernel(sorted_ref, assign_ref, out_ref):
+    rows = sorted_ref.shape[0]
+    i_row = lax.broadcasted_iota(jnp.int32, (rows, rows), 0)
+    i_col = lax.broadcasted_iota(jnp.int32, (rows, rows), 1)
+    row_values = jnp.broadcast_to(assign_ref[...], (rows, rows)).astype(jnp.float32)
+    col_values = jnp.sum(jnp.where(i_row == i_col, row_values, 0.0), axis=1, keepdims=True)
+    earlier = jnp.where(i_col < i_row, jnp.where(row_values == col_values, 1.0, 0.0), 0.0)
+    place = col_values * SAMPLES + jnp.sum(earlier, axis=1, keepdims=True)
+    back = jnp.where(i_col.astype(jnp.float32) == place, 1.0, 0.0).astype(jnp.bfloat16)
+    out_ref[...] = dot(back, sorted_ref[...]).astype(jnp.bfloat16)
+
+
 def local(size, hidden, query_key_value_weight, w_out, k_cache, value_cache, lengths, assign):
     rows, features = hidden.shape
     width = features * size
@@ -484,7 +495,7 @@
     pairs = prompts // 2
     vmem = pl.BlockSpec(memory_space=pltpu.VMEM)
     anywhere = pl.BlockSpec(memory_space=pl.ANY)
-    return pl.pallas_call(
+    finished = pl.pallas_call(
         functools.partial(layer_kernel, size, width),
         out_shape=jax.ShapeDtypeStruct((rows, features), bf16),
         in_specs=[anywhere] * 8,
@@ -542,6 +553,13 @@
         assign.reshape(1, rows),
         jnp.asarray(freq),
     )
+    return pl.pallas_call(
+        restore_kernel,
+        out_shape=jax.ShapeDtypeStruct((rows, features), bf16),
+        in_specs=[vmem, vmem],
+        out_specs=vmem,
+        name="restore",
+    )(finished, assign.reshape(1, rows))
 
 
 def solution(mesh):

time: 79.3 us -> 79.4 us (level)
  Pallas kernels: 77.6 us -> 79.2 us
  local copies, waits for them, and re-layouts: 1.53 us -> 0 us
    pallas_call x0 -> x1, Pallas kernels: none -> 1.83 us  [local(): pl.pallas_call(restore_kernel, out_shape=jax.ShapeDtypeStruct((rows, feat...]
    unnamed x1 -> x0, local copies, waits for them, and re-layouts: 1.53 us -> none
where the time goes in v6:
time: 79.4 us; the launch traced here: 79.2 us
  Pallas kernels  79.2 us (100%)
    pallas_call x1, Pallas kernels, local(): pl.pallas_call(functools.partial(layer_kernel, size, width), out_shape=ja...  77.4 us
    pallas_call x1, Pallas kernels, local(): pl.pallas_call(restore_kernel, out_shape=jax.ShapeDtypeStruct((rows, feat...  1.83 us

profile of v6, /device:TPU:20, one launch (start us, length us, event | category | flops | bytes accessed | tf_op | source)
XLA Modules:
  0.0 79.2 jit_solution(10832046113246582241)
XLA Ops:
  0.0 77.4 %layer.1.sorted_ref = bf16[64,640]{1,0:T(8,128)(2,1)} custom-call(bf16[64,640]{1,0:T(8,128)(2,1)} %x_hbm.1, bf16[40,10240]{1,0:T(8,128)(2,1)} %w_ref.1, bf16[40,8192]{1,0:T(8,128)(2,1)} %bitcast.7, bf16[8,4096,128]{2,1,0:T(8,128)(2,1)} %bitcast.5, bf16[8,4096,128]{2,1,0:T(8,128)(2,1)} %bitcast.6, s32[1,64]{1,0:T(1,128)} %bitcast.10, s32[1,64]{1,0:T(1,128)} %bitcast.8, ...), custom_call_target="tpu_custom_call" | custom-call | tf_op jit(solution)/shard_map/layer/pallas_call | solution.py:498
  77.4 1.8 %restore.1 = bf16[64,640]{1,0:T(8,128)(2,1)} custom-call(bf16[64,640]{1,0:T(8,128)(2,1)} %layer.1.sorted_ref, s32[1,64]{1,0:T(1,128)} %bitcast.9), custom_call_target="tpu_custom_call" | custom-call | tf_op jit(solution)/shard_map/restore/pallas_call | solution.py:556
